TPU v7x, 512 devices: a whole 4x8x8 slice. The times are simulated.
512 devices in a mesh: seq: 128 (over z, y, core), head: 4 (over x).
Axes of the slice: x: 4, y: 8, z: 8, core: 2. Of those that a mesh axis runs over, the one named last changes fastest.
Arguments:
- features: bfloat16 [256, 131072], P('head', 'seq'), as said below
- neighbours: int32 [2, 27, 131072], P(None, None, 'seq'), may hold values from -1 to 131071, as said below
- valid: int32 [2, 131072], P(None, 'seq'), may hold values from 0 to 1, as said below
- conv_weight: bfloat16 [2, 27, 256, 256], P(None, None, 'head'), may hold values from -0.078125 to 0.078125
- attn_weight: bfloat16 [2, 3, 256, 256], P(None, None, 'head'), as said below
- proj_weight: bfloat16 [2, 256, 256], P(None, 'head'), may hold values from -0.375 to 0.375
- hilbert_place: int32 [131072], P('seq'), may hold values from 0 to 131071, as said below
Outputs:
- output: bfloat16 [256, 131072], P('head', 'seq')
Inputs may be any that keep to these rules, and one draw needn't show every extreme that they name: `neighbours`: each entry is -1 or the index of a point within 256 positions of the point itself; tap 13 is always the point itself. The first point of every patch is valid. `hilbert_place`: A permutation of all points. Of the points on one index of seq, at most 16 go to any one index of seq in Hilbert order, and in every draw some go exactly 16; they go to 96 indices. `features`: values within -6 to 6. `attn_weight`: values within -0.2 to 0.2 at the stated sizes.
All inputs are finite; a program needn't handle non-finite values.
Results may differ from a plain program's by a relative error of at most 0.015.
Values may be sent and summed in bfloat16 or wider, within the bound.
A program may use at most 64 MiB of HBM per device.

v0:
```python
import jax
import jax.numpy as jnp
from jax import lax
from jax.sharding import PartitionSpec as P

PATCH = 1024
HD = 16
REACH = 256


def extended(shard, sides, width):
    for axis, dim in sides:
        devices, length = (lax.axis_size(axis), shard.shape[dim])
        up = [(i, (i + 1) % devices) for i in range(devices - 1)]
        down = [(j, i) for i, j in up]
        last = lax.slice_in_dim(shard, length - width, length, axis=dim)
        first = lax.slice_in_dim(shard, 0, width, axis=dim)
        before = lax.ppermute(last, axis, up)
        after = lax.ppermute(first, axis, down)
        shard = jnp.concatenate([before, shard, after], axis=dim)
    return shard


def layer_norm(values):
    mean = jnp.mean(values, axis=0, keepdims=True)
    centred = values - mean
    spread = jnp.mean(centred * centred, axis=0, keepdims=True)
    return centred * lax.rsqrt(spread + 1e-05)


def sparse_conv(table, nbrs, weight, offset):
    count = nbrs.shape[1]

    def step(tap, total):
        index = lax.dynamic_index_in_dim(nbrs, tap, 0, keepdims=False)
        local = jnp.clip(index - offset, 0, table.shape[1] - 1)
        picked = jnp.take(table, local, axis=1)
        picked = jnp.where((index >= 0)[None, :], picked, jnp.zeros_like(picked))
        kernel = lax.dynamic_index_in_dim(weight, tap, 0, keepdims=False)
        return total + jnp.dot(kernel, picked, preferred_element_type=jnp.float32)

    start = jnp.zeros((weight.shape[1], count), jnp.float32)
    return lax.fori_loop(0, 27, step, start)


def attend(query, keys, values, mask):
    width, rows = query.shape
    groups = rows // PATCH
    heads = width // HD
    scale = 1.0 / HD**0.5

    def arrange(array):
        return (
            array.reshape(heads, HD, groups, PATCH)
            .transpose(2, 0, 1, 3)
            .reshape(groups * heads, HD, PATCH)
        )

    masks = jnp.repeat(mask.reshape(groups, 1, PATCH), heads, axis=1).reshape(groups * heads, PATCH)

    def one_group(args):
        qpart, kpart, vpart, mpart = args
        scores = jnp.einsum("dq,dk->qk", qpart, kpart, preferred_element_type=jnp.float32) * scale
        scores = jnp.where(mpart[None, :] > 0, scores, -1e30)
        top = jnp.max(scores, axis=1, keepdims=True)
        weights = jnp.exp(scores - top)
        total = jnp.sum(weights, axis=1, keepdims=True)
        probs = (weights / total).astype(jnp.bfloat16)
        return jnp.einsum("dk,qk->dq", vpart, probs, preferred_element_type=jnp.float32).astype(
            jnp.bfloat16
        )

    result = lax.map(one_group, (arrange(query), arrange(keys), arrange(values), masks))
    return result.reshape(groups, heads, HD, PATCH).transpose(1, 2, 0, 3).reshape(width, rows)


def run_block(feats, nbrs, mask, conv_w, qkv_w, proj_w):
    width, rows = feats.shape
    offset = lax.axis_index("seq") * rows - REACH
    complete = lax.all_gather(feats, "head", axis=0, tiled=True)
    table = extended(complete, (("seq", 1),), REACH)
    encoded = sparse_conv(table, nbrs, conv_w, offset)
    mixed = (feats.astype(jnp.float32) + encoded).astype(jnp.bfloat16)
    whole = lax.all_gather(mixed, "head", axis=0, tiled=True)
    normed = layer_norm(whole.astype(jnp.float32)).astype(jnp.bfloat16)
    project = jnp.einsum("jdc,ct->jdt", qkv_w, normed, preferred_element_type=jnp.float32).astype(
        jnp.bfloat16
    )
    heads_out = attend(project[0], project[1], project[2], mask)
    partial_value = jnp.einsum("io,it->ot", proj_w, heads_out, preferred_element_type=jnp.float32)
    update = lax.psum_scatter(
        partial_value.astype(jnp.bfloat16), "head", scatter_dimension=0, tiled=True
    ).astype(jnp.float32)
    return (mixed.astype(jnp.float32) + update).astype(jnp.bfloat16)


def relayout(feats, places):
    width, rows = feats.shape
    shards = lax.axis_size("seq")
    room = 2 * rows // shards
    target = places // rows
    spot = places % rows
    onehot = (target[:, None] == jnp.arange(shards, dtype=jnp.int32)[None, :]).astype(jnp.int32)
    rank = jnp.sum(jnp.cumsum(onehot, axis=0) * onehot, axis=1) - 1
    slot = target * room + rank
    pointwise = feats.T
    outgoing = (
        jnp.zeros((shards * room, width), jnp.bfloat16)
        .at[slot]
        .set(pointwise)
        .reshape(shards, room * width)
    )
    spots = jnp.full((shards * room,), -1, jnp.int32).at[slot].set(spot).reshape(shards, room)
    arrived, arrived_spots = (
        lax.all_to_all(outgoing, "seq", split_axis=0, concat_axis=0, tiled=True),
        lax.all_to_all(spots, "seq", split_axis=0, concat_axis=0, tiled=True),
    )
    landing = arrived_spots.reshape(shards * room)
    landing = jnp.where(landing >= 0, landing, rows)
    result = (
        jnp.zeros((rows + 1, width), jnp.bfloat16)
        .at[landing]
        .set(arrived.reshape(shards * room, width))
    )
    return result[:rows].T


def body(features, neighbours, valid, conv_weight, attn_weight, proj_weight, hilbert_place):
    first = run_block(
        features, neighbours[0], valid[0], conv_weight[0], attn_weight[0], proj_weight[0]
    )
    moved = relayout(first, hilbert_place)
    return run_block(moved, neighbours[1], valid[1], conv_weight[1], attn_weight[1], proj_weight[1])


def solution(mesh):
    in_specs = (
        P("head", "seq"),
        P(None, None, "seq"),
        P(None, "seq"),
        P(None, None, "head", None),
        P(None, None, "head", None),
        P(None, "head", None),
        P("seq"),
    )
    out_specs = P("head", "seq")
    return jax.shard_map(body, mesh=mesh, in_specs=in_specs, out_specs=out_specs, check_vma=False)
```

profile of v0, /device:TPU:1, one launch (start us, length us, event | category | flops | bytes accessed | tf_op | source)
XLA Modules:
  0.0 523.0 jit_solution(16995070568242655883)
XLA Ops:
  6.5 11.4 %all_gather.12 = bf16[256,1024]{1,0:T(8,128)(2,1)S(1)} all-gather(bf16[64,1024]{1,0:T(8,128)(2,1)} %param.17), channel_id=1, replica_groups=mesh['seq'=128,'head'=4] {'head'}, dimensions={0}, use_global_device_ids=true | all-gather | bytes 655360 | tf_op jit(solution)/shard_map/all_gather | solution.py:80
  18.0 6.7 %collective-permute-start = (bf16[256,256]{1,0:T(8,128)(2,1)S(1)}, bf16[256,256]{1,0:T(8,128)(2,1)S(1)}, u32[]{:S(2)}, u32[]{:S(2)}) collective-permute-start(bf16[256,256]{1,0:T(8,128)(2,1)S(1)} %get-tuple-element.426), channel_id=1, source_target_pairs={{0,4},{4,8},{8,12},{12,16},{16,20},{20,24},{24,28},{28,32},{32,36}... | collective-permute-start | bytes 393224 | tf_op jit(solution)/shard_map/ppermute | solution.py:18
  24.6 5.1 collective-permute-start.1
  35.5 184.1 %while.50 = (s32[]{:T(128)}, f32[64,1024]{1,0:T(8,128)}, bf16[27,64,256]{2,1,0:T(8,128)(2,1)S(1)}, s32[27,1024]{1,0:T(8,128)}, s32[]{:T(128)}, /*index=5*/bf16[256,1536]{0,1:T(8,128)(2,1)S(1)}, s32[]{:T(128)}, s32[]{:T(128)}) while((s32[]{:T(128)}, f32[64,1024]{1,0:T(8,128)}, bf16[27,64,256]{2,1,0:T(8,128)(2,1)S(1)}, ...), condition=%wide.region_5.7_spmd.clone, body=%wide.region_4.6_spmd.clone.sunk | while | flops 34223104 | bytes 4260007 | solution.py:43
  36.3 3.9 gather_fusion
  43.1 3.9 gather_fusion
  50.0 3.9 gather_fusion
  56.8 3.9 gather_fusion
  63.6 3.9 gather_fusion
  220.5 11.6 %all_gather.13 = bf16[256,1024]{1,0:T(8,128)(2,1)S(1)} all-gather(bf16[64,1024]{1,0:T(8,128)(2,1)S(1)} %add_convert_fusion.3), channel_id=1, replica_groups=mesh['seq'=128,'head'=4] {'head'}, dimensions={0}, use_global_device_ids=true | all-gather | bytes 655360 | tf_op jit(solution)/shard_map/all_gather | solution.py:84
  233.7 11.7 %while.48 = (s32[]{:T(128)}, bf16[4,16,1024]{2,1,0:T(8,128)(2,1)S(1)}, bf16[4,16,1024]{2,1,0:T(8,128)(2,1)S(1)}, s32[4,1024]{1,0:T(4,128)S(1)}, bf16[4,16,1024]{...) while((s32[]{:T(128)}, bf16[4,16,1024]{2,1,0:T(8,128)(2,1)S(1)}, ...), condition=%wide.region_11.13_spmd, body=%wide.region_8.12_spmd.sunk | while | flops 79707136 | bytes 12744785 | solution.py:73
  247.6 4.5 scatter_custom_fusion
  252.8 17.3 %all-to-all-start = ((s32[128,1,16]{2,1,0:T(1,128)}), s32[128,1,16]{2,1,0:T(1,128)S(1)}, u32[]{:S(2)}, u32[]{:S(2)}) async-start(s32[128,1,16]{2,1,0:T(1,128)} %bitcast.12), calls=%async_computation | async-start | bytes 131072 | tf_op jit(solution)/shard_map/all_to_all | solution.py:116
  270.1 5.9 %reduce-scatter.7.cloned.1.call-done = bf16[64,1024]{1,0:T(8,128)(2,1)} async-done(((bf16[256,1024]{1,0:T(8,128)(2,1)}), bf16[64,1024]{1,0:T(8,128)(2,1)}) %reduce-scatter.7.cloned.1.call-update) | async-done | bytes 131088 | tf_op jit(solution)/shard_map/reduce_scatter | solution.py:91
  284.5 15.7 %all-to-all-start.1 = ((bf16[128,2,512]{2,1,0:T(2,128)(2,1)}), bf16[128,2,512]{2,1,0:T(2,128)(2,1)S(1)}, u32[]{:S(2)}, u32[]{:S(2)}) async-start(bf16[128,2,512]{2,1,0:T(2,128)(2,1)} %reshape.182), calls=%async_computation.1 | async-start | bytes 524288 | tf_op jit(solution)/shard_map/all_to_all | solution.py:115
  301.6 13.8 %all-to-all-done.1 = bf16[128,2,512]{2,1,0:T(2,128)(2,1)S(1)} async-done(((bf16[128,2,512]{2,1,0:T(2,128)(2,1)}), bf16[128,2,512]{2,1,0:T(2,128)(2,1)S(1)}, u32[]{:S(2)}, u32[]{:S(2)}) %all-to-all-start.1) | async-done | bytes 262176 | tf_op jit(solution)/shard_map/all_to_all | solution.py:115
  317.6 5.8 %scatter_custom_fusion.2 = bf16[1025,64]{1,0:T(8,128)(2,1)S(1)} fusion(s32[2048]{0:T(1024)S(1)} %bitcast.158, bf16[2048,64]{1,0:T(8,128)(2,1)S(1)} %reshape.144, bf16[]{:T(256)} %constant.183.clone.1), kind=kCustom, calls=%fused_computation.125 | custom fusion | bytes 131202 | tf_op jit(solution)/shard_map/scatter | solution.py:123
  323.5 9.9 %all_gather.14 = bf16[256,1024]{1,0:T(8,128)(2,1)S(1)} all-gather(bf16[64,1024]{1,0:T(8,128)(2,1)S(1)} %bitcast.141), channel_id=1, replica_groups=mesh['seq'=128,'head'=4] {'head'}, dimensions={0}, use_global_device_ids=true | all-gather | bytes 655360 | tf_op jit(solution)/shard_map/all_gather | solution.py:80
  333.5 6.6 %collective-permute-start.2 = (bf16[256,256]{1,0:T(8,128)(2,1)S(1)}, bf16[256,256]{1,0:T(8,128)(2,1)S(1)}, u32[]{:S(2)}, u32[]{:S(2)}) collective-permute-start(bf16[256,256]{1,0:T(8,128)(2,1)S(1)} %get-tuple-element.424), channel_id=1, source_target_pairs={{0,4},{4,8},{8,12},{12,16},{16,20},{20,24},{24,28},{28,32},{32,36}... | collective-permute-start | bytes 393224 | tf_op jit(solution)/shard_map/ppermute | solution.py:18
  342.0 4.3 collective-permute-done.3
  346.7 123.7 %while.51 = (s32[]{:T(128)}, f32[64,1024]{1,0:T(8,128)S(1)}, bf16[27,64,256]{2,1,0:T(8,128)(2,1)S(1)}, s32[27,1024]{1,0:T(8,128)S(1)}, s32[]{:T(128)}, /*index=5*/bf16[256,1536]{0,1:T(8,128)(2,1)S(1)}, s32[]{:T(128)}, s32[]{:T(128)}) while((s32[]{:T(128)}, f32[64,1024]{1,0:T(8,128)S(1)}, bf16[27,64,256]{2,1,0:T(8,128)(2,1)S(1)}, ...), condition=%wide.region_16.18_spmd.clone, body=%wide.region_15.17_spmd.clone.sunk | while | flops 34223104 | bytes 2162799 | solution.py:43
  470.4 11.1 %all_gather.15 = bf16[256,1024]{1,0:T(8,128)(2,1)S(1)} all-gather(bf16[64,1024]{1,0:T(8,128)(2,1)S(1)} %add_convert_fusion.1), channel_id=1, replica_groups=mesh['seq'=128,'head'=4] {'head'}, dimensions={0}, use_global_device_ids=true | all-gather | bytes 655360 | tf_op jit(solution)/shard_map/all_gather | solution.py:84
  482.2 11.7 %while.49 = (s32[]{:T(128)}, bf16[4,16,1024]{2,1,0:T(8,128)(2,1)S(1)}, bf16[4,16,1024]{2,1,0:T(8,128)(2,1)S(1)}, s32[4,1024]{1,0:T(4,128)S(1)}, bf16[4,16,1024]{...) while((s32[]{:T(128)}, bf16[4,16,1024]{2,1,0:T(8,128)(2,1)S(1)}, ...), condition=%wide.region_22.24_spmd, body=%wide.region_19.23_spmd.sunk | while | flops 79707136 | bytes 12744785 | solution.py:73
  495.2 19.4 %reduce-scatter.9.cloned.1.call-done = bf16[64,1024]{1,0:T(8,128)(2,1)} async-done(((bf16[256,1024]{1,0:T(8,128)(2,1)}), bf16[64,1024]{1,0:T(8,128)(2,1)}) %reduce-scatter.9.cloned.1.call-update) | async-done | bytes 131088 | tf_op jit(solution)/shard_map/reduce_scatter | solution.py:91
  (547 shorter events, 337.4 us)
Async XLA Ops:
  6.5 24.9 %copy-start.4 = (s32[2,27,1024]{2,0,1:T(2,128)S(1)}, s32[2,27,1024]{2,0,1:T(2,128)}, u32[]{:S(2)}) copy-start(s32[2,27,1024]{2,0,1:T(2,128)} %param.18) | copy-start | bytes 663556
  6.5 26.4 %copy-start.8 = (s32[1024]{0:T(1024)S(1)}, s32[1024]{0:T(1024)}, u32[]{:S(2)}) copy-start(s32[1024]{0:T(1024)} %param.23) | copy-start | bytes 12292
  6.5 27.1 %copy-start.7 = (s32[2,1024]{1,0:T(2,128)S(1)}, s32[2,1024]{1,0:T(2,128)}, u32[]{:S(2)}) copy-start(s32[2,1024]{1,0:T(2,128)} %param.19) | copy-start | bytes 24580
  6.5 269.4 %reduce-scatter.7.cloned.1.call-start = ((), (), s32[]{:S(2)}) async-start(), calls=%async_computation.4 | async-start | bytes 655360 | tf_op jit(solution)/shard_map/reduce_scatter | solution.py:91
  18.0 16.2 %collective-permute-start = (bf16[256,256]{1,0:T(8,128)(2,1)S(1)}, bf16[256,256]{1,0:T(8,128)(2,1)S(1)}, u32[]{:S(2)}, u32[]{:S(2)}) collective-permute-start(bf16[256,256]{1,0:T(8,128)(2,1)S(1)} %get-tuple-element.426), channel_id=1, source_target_pairs={{0,4},{4,8},{8,12},{12,16},{16,20},{20,24},{24,28},{28,32},{32,36}... | collective-permute-start | bytes 393224 | tf_op jit(solution)/shard_map/ppermute | solution.py:18
  24.6 9.6 %collective-permute-start.1 = (bf16[256,256]{1,0:T(8,128)(2,1)S(1)}, bf16[256,256]{1,0:T(8,128)(2,1)}, u32[]{:S(2)}, u32[]{:S(2)}) collective-permute-start(bf16[256,256]{1,0:T(8,128)(2,1)S(1)} %get-tuple-element.427), channel_id=1, source_target_pairs={{4,0},{8,4},{12,8},{16,12},{20,16},{24,20},{28,24},{32,28},{36,32}... | collective-permute-start | bytes 393224 | tf_op jit(solution)/shard_map/ppermute | solution.py:19
  35.4 184.1 %copy-start = (bf16[64,1024]{1,0:T(8,128)(2,1)S(1)}, bf16[64,1024]{1,0:T(8,128)(2,1)}, u32[]{:S(2)}) copy-start(bf16[64,1024]{1,0:T(8,128)(2,1)} %param.17) | copy-start | bytes 393220
  35.5 5.6 %copy-start.2 = (f32[64,1024]{1,0:T(8,128)S(1)}, f32[64,1024]{1,0:T(8,128)}, u32[]{:S(2)}) copy-start(f32[64,1024]{1,0:T(8,128)} %get-tuple-element.605) | copy-start | bytes 786436 | tf_op jit(solution)/shard_map/while
  42.3 5.6 %copy-start.2 = (f32[64,1024]{1,0:T(8,128)S(1)}, f32[64,1024]{1,0:T(8,128)}, u32[]{:S(2)}) copy-start(f32[64,1024]{1,0:T(8,128)} %get-tuple-element.605) | copy-start | bytes 786436 | tf_op jit(solution)/shard_map/while
  55.9 5.6 %copy-start.2 = (f32[64,1024]{1,0:T(8,128)S(1)}, f32[64,1024]{1,0:T(8,128)}, u32[]{:S(2)}) copy-start(f32[64,1024]{1,0:T(8,128)} %get-tuple-element.605) | copy-start | bytes 786436 | tf_op jit(solution)/shard_map/while
  62.8 5.6 %copy-start.2 = (f32[64,1024]{1,0:T(8,128)S(1)}, f32[64,1024]{1,0:T(8,128)}, u32[]{:S(2)}) copy-start(f32[64,1024]{1,0:T(8,128)} %get-tuple-element.605) | copy-start | bytes 786436 | tf_op jit(solution)/shard_map/while
  76.4 5.6 %copy-start.2 = (f32[64,1024]{1,0:T(8,128)S(1)}, f32[64,1024]{1,0:T(8,128)}, u32[]{:S(2)}) copy-start(f32[64,1024]{1,0:T(8,128)} %get-tuple-element.605) | copy-start | bytes 786436 | tf_op jit(solution)/shard_map/while
  83.2 5.6 %copy-start.2 = (f32[64,1024]{1,0:T(8,128)S(1)}, f32[64,1024]{1,0:T(8,128)}, u32[]{:S(2)}) copy-start(f32[64,1024]{1,0:T(8,128)} %get-tuple-element.605) | copy-start | bytes 786436 | tf_op jit(solution)/shard_map/while
  90.0 5.6 %copy-start.2 = (f32[64,1024]{1,0:T(8,128)S(1)}, f32[64,1024]{1,0:T(8,128)}, u32[]{:S(2)}) copy-start(f32[64,1024]{1,0:T(8,128)} %get-tuple-element.605) | copy-start | bytes 786436 | tf_op jit(solution)/shard_map/while
  96.8 5.6 %copy-start.2 = (f32[64,1024]{1,0:T(8,128)S(1)}, f32[64,1024]{1,0:T(8,128)}, u32[]{:S(2)}) copy-start(f32[64,1024]{1,0:T(8,128)} %get-tuple-element.605) | copy-start | bytes 786436 | tf_op jit(solution)/shard_map/while
  219.5 14.1 %copy-start.6 = (s32[1,1024]{1,0:T(1,128)S(1)}, s32[1,1024]{1,0:T(1,128)}, u32[]{:S(2)}) copy-start(s32[1,1024]{1,0:T(1,128)} %get-tuple-element.437) | copy-start | bytes 12292
  233.7 11.7 %copy-start.5 = (bf16[2,64,256]{2,1,0:T(8,128)(2,1)S(1)}, bf16[2,64,256]{2,1,0:T(8,128)(2,1)}, u32[]{:S(2)}) copy-start(bf16[2,64,256]{2,1,0:T(8,128)(2,1)} %param.22) | copy-start | bytes 196612
  252.8 31.7 %all-to-all-start = ((s32[128,1,16]{2,1,0:T(1,128)}), s32[128,1,16]{2,1,0:T(1,128)S(1)}, u32[]{:S(2)}, u32[]{:S(2)}) async-start(s32[128,1,16]{2,1,0:T(1,128)} %bitcast.12), calls=%async_computation | async-start | bytes 131072 | tf_op jit(solution)/shard_map/all_to_all | solution.py:116
  277.1 64.9 %copy-start.1 = (s32[1,27,1024]{2,0,1:T(1,128)S(1)}, s32[1,27,1024]{2,0,1:T(1,128)}, u32[]{:S(2)}) copy-start(s32[1,27,1024]{2,0,1:T(1,128)} %get-tuple-element.435) | copy-start | bytes 331780
  284.5 30.9 %all-to-all-start.1 = ((bf16[128,2,512]{2,1,0:T(2,128)(2,1)}), bf16[128,2,512]{2,1,0:T(2,128)(2,1)S(1)}, u32[]{:S(2)}, u32[]{:S(2)}) async-start(bf16[128,2,512]{2,1,0:T(2,128)(2,1)} %reshape.182), calls=%async_computation.1 | async-start | bytes 524288 | tf_op jit(solution)/shard_map/all_to_all | solution.py:115
  300.1 214.5 %reduce-scatter.9.cloned.1.call-start = ((), (), s32[]{:S(2)}) async-start(), calls=%async_computation.5 | async-start | bytes 655360 | tf_op jit(solution)/shard_map/reduce_scatter | solution.py:91
  333.5 8.5 %collective-permute-start.2 = (bf16[256,256]{1,0:T(8,128)(2,1)S(1)}, bf16[256,256]{1,0:T(8,128)(2,1)S(1)}, u32[]{:S(2)}, u32[]{:S(2)}) collective-permute-start(bf16[256,256]{1,0:T(8,128)(2,1)S(1)} %get-tuple-element.424), channel_id=1, source_target_pairs={{0,4},{4,8},{8,12},{12,16},{16,20},{20,24},{24,28},{28,32},{32,36}... | collective-permute-start | bytes 393224 | tf_op jit(solution)/shard_map/ppermute | solution.py:18
  340.0 6.3 %collective-permute-start.3 = (bf16[256,256]{1,0:T(8,128)(2,1)S(1)}, bf16[256,256]{1,0:T(8,128)(2,1)S(1)}, u32[]{:S(2)}, u32[]{:S(2)}) collective-permute-start(bf16[256,256]{1,0:T(8,128)(2,1)S(1)} %get-tuple-element.425), channel_id=1, source_target_pairs={{4,0},{8,4},{12,8},{16,12},{20,16},{24,20},{28,24},{32,28},{36,32}... | collective-permute-start | bytes 393224 | tf_op jit(solution)/shard_map/ppermute | solution.py:19
  346.6 135.1 %copy-start.9 = (bf16[2,3,64,256]{3,2,1,0:T(8,128)(2,1)S(1)}, bf16[2,3,64,256]{3,2,1,0:T(8,128)(2,1)}, u32[]{:S(2)}) copy-start(bf16[2,3,64,256]{3,2,1,0:T(8,128)(2,1)} %param.21) | copy-start | bytes 589828
  (46 other events, 124.9 us)
Sparse Core Ops, SparseCore 0:
  246.9 28.9 reduce-scatter.6
  495.4 19.2 reduce-scatter.8
where the time goes:
time: 527 us; the launch traced here: 523 us
  local copies, waits for them, and re-layouts  256 us (49%)
  other arithmetic  63.9 us (12%)
  starting transfers between devices  53.3 us (10%)
  matrix products  45.9 us (9%)
  blocking collectives  44 us (8%)
  waiting for transfers between devices  43.3 us (8%)
  between operations  13.8 us (3%)
    gather x54, local copies, waits for them, and re-layouts, step(): picked = jnp.take(table, local, axis=1)  213 us
    dot_general x54, matrix products, step(): return total + jnp.dot(kernel, picked, preferred_element_type=jnp.float32)  28 us
    reduce_scatter x2, waiting for transfers between devices, run_block(): lax.psum_scatter(partial_value.astype(jnp.bfloat16), 'head', scatter_dime...  25.2 us
    all_gather x2, blocking collectives, run_block(): whole = lax.all_gather(mixed, 'head', axis=0, tiled=True)  22.7 us
    min x54, other arithmetic, step(): local = jnp.clip(index - offset, 0, table.shape[1] - 1)  22.4 us
    ge x54, other arithmetic, step(): picked = jnp.where((index >= 0)[None, :], picked, jnp.zeros_like(picked))  22.2 us
    all_gather x2, blocking collectives, run_block(): complete = lax.all_gather(feats, 'head', axis=0, tiled=True)  21.3 us
    while x108, local copies, waits for them, and re-layouts  18.5 us
  transfers between devices with their start and end apart: 8, of which 4 were waited for; matrix products, arithmetic and copies ran while one was open for 4% of the time, Pallas kernels for 0%

commit v1 on v0

v1 whole, which is shorter than its diff:
```python
import functools

import jax
import jax.numpy as jnp
from jax import lax
from jax.experimental import pallas as pl
from jax.experimental.pallas import tpu as pltpu
from jax.sharding import PartitionSpec as P

PATCH = 1024
HD = 16
REACH = 256
TAPS = 27
CAP = 16
MESH = pl.DeviceIdType.MESH
BF16 = jnp.bfloat16
F32 = jnp.float32


def remote(src, dst, send, recv, s, h):
    return pltpu.make_async_remote_copy(
        src_ref=src,
        dst_ref=dst,
        send_sem=send,
        recv_sem=recv,
        device_id=(s, h),
        device_id_type=MESH,
    )


def block_kernel(
    block,
    x,
    nbr,
    valid,
    cw,
    aw,
    pw,
    out,
    table,
    nb,
    vm,
    w,
    a,
    p,
    y,
    mix,
    kt,
    qm,
    va,
    ho,
    pt,
    local,
    s1,
    r1,
    s2,
    r2,
    s3,
    r3,
    s4,
    r4,
    s5,
    r5,
):
    width, rows = out.shape
    heads = width // HD
    groups = lax.axis_size("head")
    shards = lax.axis_size("seq")
    s = lax.axis_index("seq")
    h = lax.axis_index("head")
    after = lax.rem(s + 1, shards)
    before = lax.rem(s + shards - 1, shards)
    peers = [lax.rem(h + d, groups) for d in range(1, groups)]
    froms = [lax.rem(h + groups - d, groups) for d in range(1, groups)]
    blocks = rows // REACH

    def part(index, size=width, extra=0):
        return pl.ds(pl.multiple_of(index * width + extra, 16), size)

    mine = part(h)

    barrier = pltpu.get_barrier_semaphore()
    for other in peers:
        pl.semaphore_signal(barrier, inc=1, device_id=(s, other), device_id_type=MESH)
    for other in (before, after):
        pl.semaphore_signal(barrier, inc=1, device_id=(other, h), device_id_type=MESH)
    loads = [
        pltpu.make_async_copy(x, table.at[mine, pl.ds(REACH, rows)], local.at[0]),
        pltpu.make_async_copy(nbr.at[block], nb, local.at[1]),
        pltpu.make_async_copy(valid, vm, local.at[2]),
        pltpu.make_async_copy(cw.at[block], w, local.at[3]),
        pltpu.make_async_copy(aw.at[block], a, local.at[4]),
        pltpu.make_async_copy(pw.at[block], p.at[mine, :], local.at[5]),
    ]
    for load in loads:
        load.start()
    pl.semaphore_wait(barrier, groups + 1)

    pieces = ((0, REACH), (rows - REACH, REACH), (REACH, rows - 2 * REACH))
    sends = []
    for j, (low, size) in enumerate(pieces):
        for d, other in enumerate(peers):
            copy = remote(
                x.at[:, pl.ds(low, size)],
                table.at[mine, pl.ds(REACH + low, size)],
                s1.at[j, d],
                r1.at[j, d],
                s,
                other,
            )
            copy.start()
            sends.append(copy)

    def arrived(j):
        low, size = pieces[j]
        for d, other in enumerate(froms):
            remote(
                x.at[:, pl.ds(low, size)],
                table.at[part(other), pl.ds(REACH + low, size)],
                s1.at[j, d],
                r1.at[j, d],
                s,
                other,
            ).wait_recv()

    loads[0].wait()
    arrived(0)
    first = remote(
        table.at[:, pl.ds(REACH, REACH)],
        table.at[:, pl.ds(REACH + rows, REACH)],
        s2.at[0],
        r2.at[0],
        before,
        h,
    )
    first.start()
    arrived(1)
    last = remote(
        table.at[:, pl.ds(rows, REACH)],
        table.at[:, pl.ds(0, REACH)],
        s2.at[1],
        r2.at[1],
        after,
        h,
    )
    last.start()
    sends += [first, last]
    loads[5].wait()
    for d, other in enumerate(peers):
        copy = remote(p.at[mine, :], p.at[mine, :], s5.at[d], r5.at[d], s, other)
        copy.start()
        sends.append(copy)
    for load in loads[1:5]:
        load.wait()
    arrived(2)

    step = 9

    def products(tile):
        points = table[:, tile * REACH : (tile + 1) * REACH]

        def some(i, carry):
            taps = w[pl.ds(i * step, step)].reshape(step * width, -1)
            value = jnp.dot(taps, points, preferred_element_type=F32).astype(BF16)
            y[pl.ds(i * step, step), tile] = value.reshape(step, width, REACH)
            return carry

        lax.fori_loop(0, TAPS // step, some, 0)

    for tile in range(1, blocks + 1):
        products(tile)
    first.wait_recv()
    last.wait_recv()
    products(0)
    products(blocks + 1)

    place = lax.broadcasted_iota(jnp.int32, (REACH, REACH), 0)
    for blk in range(blocks):
        cols = slice(blk * REACH, (blk + 1) * REACH)
        base = s * rows + (blk - 1) * REACH

        def tap(t, total):
            index = nb[pl.ds(t, 1), cols]
            spot = index - base
            tile = jnp.where(index < 0, 3, spot >> 8)
            pick = (place == (spot & (REACH - 1))).astype(F32).astype(BF16)
            terms = y[t, blk : blk + 3].reshape(3 * width, REACH)
            picked = jnp.dot(terms, pick, preferred_element_type=F32)
            term = jnp.where(tile == 0, picked[:width], 0.0)
            term = jnp.where(tile == 1, picked[width : 2 * width], term)
            term = jnp.where(tile == 2, picked[2 * width :], term)
            return total + term

        total = lax.fori_loop(0, TAPS, tap, jnp.zeros((width, REACH), F32), unroll=3)
        own = table[mine, REACH + blk * REACH : REACH + (blk + 1) * REACH].astype(F32)
        mix[mine, cols] = (own + total).astype(BF16)
        for d, other in enumerate(peers):
            copy = remote(mix.at[mine, cols], mix.at[mine, cols], s3.at[blk, d], r3.at[blk, d], s, other)
            copy.start()
            sends.append(copy)

    scale = 1.0 / HD**0.5
    bias = jnp.where(vm[block : block + 1, :] > 0, 0.0, -1e30)
    ones = jnp.where(lax.broadcasted_iota(jnp.int32, (HD, rows), 0) == 0, 1.0, 0.0).astype(BF16)
    qm[...] = jnp.zeros(qm.shape, BF16)
    for hd in range(heads):
        qm[hd, width : width + HD, :] = ones
        va[hd, HD:, :] = ones
    weights = a[...].reshape(3 * width, -1)
    for blk in range(blocks):
        cols = slice(blk * REACH, (blk + 1) * REACH)
        for d, other in enumerate(froms):
            theirs = mix.at[part(other), cols]
            remote(theirs, theirs, s3.at[blk, d], r3.at[blk, d], s, other).wait_recv()
        values = mix[:, cols].astype(F32)
        centred = values - jnp.mean(values, axis=0, keepdims=True)
        spread = jnp.mean(centred * centred, axis=0, keepdims=True)
        normed = (centred * lax.rsqrt(spread + 1e-05)).astype(BF16)
        qkv = jnp.dot(weights, normed, preferred_element_type=F32)
        query = (qkv[:width].astype(BF16).astype(F32) * scale).astype(BF16)
        value = qkv[2 * width :].astype(BF16)
        for hd in range(heads):
            span = slice(hd * HD, (hd + 1) * HD)
            qm[hd, span, cols] = query[span]
            va[hd, :HD, cols] = value[span]
        tail = jnp.where(
            lax.broadcasted_iota(jnp.int32, (width, REACH), 0) == 0, bias[:, cols], 0.0
        )
        keys = jnp.concatenate([qkv[width : 2 * width], tail], axis=0)
        kt[cols, :] = keys.T.astype(BF16)

    for d, other in enumerate(froms):
        theirs = p.at[part(other), :]
        remote(theirs, theirs, s5.at[d], r5.at[d], s, other).wait_recv()
    pt[...] = p[...].astype(F32).T.astype(BF16)

    for hd in range(heads):
        for blk in range(blocks):
            cols = slice(blk * REACH, (blk + 1) * REACH)
            scores = jnp.dot(kt[...], qm[hd, :, cols], preferred_element_type=F32)
            top = jnp.max(scores, axis=0, keepdims=True)
            probs = jnp.exp(scores - top).astype(BF16)
            summed = jnp.dot(va[hd], probs, preferred_element_type=F32)
            result = summed[:HD] / summed[HD : HD + 1]
            ho[part(h, HD, hd * HD), cols] = result.astype(BF16)
        span = part(h, HD, hd * HD)
        for d, other in enumerate(peers):
            copy = remote(ho.at[span, :], ho.at[span, :], s4.at[hd, d], r4.at[hd, d], s, other)
            copy.start()
            sends.append(copy)
    for hd in range(heads):
        for d, other in enumerate(froms):
            theirs = ho.at[part(other, HD, hd * HD), :]
            remote(theirs, theirs, s4.at[hd, d], r4.at[hd, d], s, other).wait_recv()
    update = jnp.dot(pt[mine, :], ho[...], preferred_element_type=F32)
    out[...] = (mix[mine, :].astype(F32) + update).astype(BF16)
    for copy in sends:
        copy.wait_send()


def run_block(block, groups, x, nbr, valid, cw, aw, pw):
    width, rows = x.shape
    channels = width * groups
    heads = width // HD
    blocks = rows // REACH
    others = groups - 1
    dma = pltpu.SemaphoreType.DMA
    return pl.pallas_call(
        functools.partial(block_kernel, block),
        out_shape=jax.ShapeDtypeStruct((width, rows), BF16),
        in_specs=[pl.BlockSpec(memory_space=pl.ANY)] * 6,
        out_specs=pl.BlockSpec(memory_space=pltpu.VMEM),
        scratch_shapes=[
            pltpu.VMEM((channels, rows + 2 * REACH), BF16),
            pltpu.VMEM((TAPS, rows), jnp.int32),
            pltpu.VMEM((2, rows), jnp.int32),
            pltpu.VMEM((TAPS, width, channels), BF16),
            pltpu.VMEM((3, width, channels), BF16),
            pltpu.VMEM((channels, channels), BF16),
            pltpu.VMEM((TAPS, blocks + 2, width, REACH), BF16),
            pltpu.VMEM((channels, rows), BF16),
            pltpu.VMEM((rows, 2 * width), BF16),
            pltpu.VMEM((heads, 2 * width, rows), BF16),
            pltpu.VMEM((heads, 2 * HD, rows), BF16),
            pltpu.VMEM((channels, rows), BF16),
            pltpu.VMEM((channels, channels), BF16),
            dma((6,)),
            dma((3, others)),
            dma((3, others)),
            dma((2,)),
            dma((2,)),
            dma((blocks, others)),
            dma((blocks, others)),
            dma((heads, others)),
            dma((heads, others)),
            dma((others,)),
            dma((others,)),
        ],
        compiler_params=pltpu.CompilerParams(
            collective_id=block, has_side_effects=True, vmem_limit_bytes=48 * 2**20
        ),
        name=f"block{block}",
    )(x, nbr, valid, cw, aw, pw)


def order_kernel(x, places, out, pv, feats, tri, pick, going, come, land, flat, turned, local, s1, r1, s2, r2):
    width, rows = x.shape
    chips = places.shape[0]
    lines = places.shape[1]
    lanes = places.shape[2]
    s = lax.axis_index("seq")
    h = lax.axis_index("head")
    core = lax.rem(s, 2)
    chip = s // 2
    sibling = s + 1 - 2 * core

    barrier = pltpu.get_barrier_semaphore()

    def greet(i, carry):
        other = lax.rem(chip + i, chips) * 2 + core
        pl.semaphore_signal(barrier, inc=1, device_id=(other, h), device_id_type=MESH)
        return carry

    pl.semaphore_signal(barrier, inc=1, device_id=(sibling, h), device_id_type=MESH)
    lax.fori_loop(1, chips, greet, 0)
    load = pltpu.make_async_copy(places, pv, local.at[0])
    load.start()
    keep = pltpu.make_async_copy(x, feats.at[core], local.at[1])
    keep.start()
    load.wait()
    pl.semaphore_wait(barrier, chips)
    swap = remote(x, feats.at[core], s1.at[0], r1.at[0], sibling, h)
    swap.start()

    low = lax.broadcasted_iota(jnp.int32, (lanes, lanes), 0)
    high = lax.broadcasted_iota(jnp.int32, (lanes, lanes), 1)
    tri[...] = jnp.where(low <= high, 1.0, 0.0).astype(BF16)

    column = lax.broadcasted_iota(jnp.int32, (chips, lanes), 0)
    run = jnp.zeros((chips, 1), F32)
    slots = []
    for line in range(lines):
        row = pv[chip, line : line + 1, :]
        device = row // rows
        mask = jnp.where(device == column * 2 + core, 1.0, 0.0)
        counts = jnp.dot(mask.astype(BF16), tri[...], preferred_element_type=F32) + run
        run = counts[:, lanes - 1 :]
        rank = (jnp.sum(mask * counts, axis=0, keepdims=True) - 1.0).astype(jnp.int32)
        here = lax.rem(device, 2) == core
        target = (device // 2) * CAP + (rank & (CAP - 1))
        slots.append((jnp.where(here, target, -1), rank // CAP))
    targets = jnp.concatenate([t for t, _ in slots], axis=1)
    halves = jnp.concatenate([e for _, e in slots], axis=1)
    for e in range(2):
        pick[e : e + 1, :] = jnp.where(halves == e, targets, -1)

    keep.wait()
    swap.wait_recv()
    points = jnp.concatenate([feats[0], feats[1]], axis=1)
    strip = 16 * CAP
    strips = chips // 16
    own = chip // 16
    spot = lax.broadcasted_iota(jnp.int32, (strip, 2 * rows), 0)
    nt = (((1,), (1,)), ((), ()))

    def sort(i, carry):
        which = lax.rem(own + i, strips)
        sides = []
        for e in range(2):
            onehot = (spot + which * strip == pick[e : e + 1, :]).astype(F32).astype(BF16)
            sides.append(lax.dot_general(onehot, points, nt, preferred_element_type=F32))
        both = jnp.concatenate(sides, axis=1).astype(BF16)
        going[pl.ds(which * 16, 16)] = both.reshape(16, CAP, 2 * width)

        def send(j, c):
            other = which * 16 + lax.rem(chip + j, 16)

            @pl.when(other != chip)
            def _():
                remote(going.at[other], come.at[chip], s2.at[0], r2.at[0], other * 2 + core, h).start()

            return c

        lax.fori_loop(0, 16, send, 0)
        return carry

    lax.fori_loop(0, strips, sort, 0)
    stay = pltpu.make_async_copy(going.at[chip], come.at[chip], local.at[2])
    stay.start()

    run = jnp.zeros((chips, 1), F32)
    for line in range(lines):
        row = pv[:, line, :]
        mask = jnp.where(row // rows == s, 1.0, 0.0)
        counts = jnp.dot(mask.astype(BF16), tri[...], preferred_element_type=F32) + run
        run = counts[:, lanes - 1 :]
        land[line] = jnp.where(mask > 0, counts - 1.0, -1.0)
        flat[line] = ((row & (rows - 1)) + 1).astype(F32)
    where = lax.broadcasted_iota(jnp.int32, (chips, rows), 1).astype(F32) + 1.0

    def settle(k, carry):
        found = jnp.zeros((chips, lanes), F32)
        for line in range(lines):
            found += jnp.where(land[line] == k.astype(F32), flat[line], 0.0)
        spots = jnp.sum(found, axis=1, keepdims=True)
        turned[pl.ds(pl.multiple_of(k * chips, 16), chips), :] = (spots == where).astype(F32).astype(BF16)
        return carry

    lax.fori_loop(0, 2 * CAP, settle, 0)

    stay.wait()
    many = pl.ds(0, chips - 1)
    every = remote(going.at[many], come.at[many], s2.at[0], r2.at[0], sibling, h)
    every.wait_recv()
    arrived = come[...].astype(F32)
    parts = []
    for k in range(0, CAP, 2):
        two = jnp.concatenate([arrived[:, k, :], arrived[:, k + 1, :]], axis=0)
        parts.append(two.T.astype(BF16))
    packed = jnp.concatenate(parts, axis=1)
    half = CAP * chips
    total = jnp.dot(packed[:width], turned[:half, :], preferred_element_type=F32)
    total += jnp.dot(packed[width:], turned[half:, :], preferred_element_type=F32)
    out[...] = total.astype(BF16)
    swap.wait_send()
    every.wait_send()


def change_order(x, places):
    width, rows = x.shape
    chips, lines, lanes = places.shape
    dma = pltpu.SemaphoreType.DMA
    return pl.pallas_call(
        order_kernel,
        out_shape=jax.ShapeDtypeStruct((width, rows), BF16),
        in_specs=[pl.BlockSpec(memory_space=pl.ANY)] * 2,
        out_specs=pl.BlockSpec(memory_space=pltpu.VMEM),
        scratch_shapes=[
            pltpu.VMEM((chips, lines, lanes), jnp.int32),
            pltpu.VMEM((2, width, rows), BF16),
            pltpu.VMEM((lanes, lanes), BF16),
            pltpu.VMEM((2, 2 * rows), jnp.int32),
            pltpu.VMEM((chips, CAP, 2 * width), BF16),
            pltpu.VMEM((chips, CAP, 2 * width), BF16),
            pltpu.VMEM((lines, chips, lanes), F32),
            pltpu.VMEM((lines, chips, lanes), F32),
            pltpu.VMEM((2 * CAP * chips, rows), BF16),
            dma((3,)),
            dma((1,)),
            dma((1,)),
            dma((1,)),
            dma((1,)),
        ],
        compiler_params=pltpu.CompilerParams(
            collective_id=2, has_side_effects=True, vmem_limit_bytes=48 * 2**20
        ),
        name="change_order",
    )(x, places)


def body(groups, features, neighbours, valid, conv_weight, attn_weight, proj_weight, hilbert_place):
    rows = hilbert_place.shape[0]
    places = lax.all_gather(hilbert_place.reshape(1, rows // 128, 128), "seq", axis=0, tiled=True)
    shards = places.shape[0]
    places = places.reshape(shards // 2, rows // 64, 128)
    rest = (neighbours, valid, conv_weight, attn_weight, proj_weight)
    first = run_block(0, groups, features, *rest)
    moved = change_order(first, places)
    return run_block(1, groups, moved, *rest)


def solution(mesh):
    in_specs = (
        P("head", "seq"),
        P(None, None, "seq"),
        P(None, "seq"),
        P(None, None, "head", None),
        P(None, None, "head", None),
        P(None, "head", None),
        P("seq"),
    )
    out_specs = P("head", "seq")
    return jax.shard_map(
        functools.partial(body, mesh.shape["head"]),
        mesh=mesh,
        in_specs=in_specs,
        out_specs=out_specs,
        check_vma=False,
    )
```

time: 527 us -> 179 us (0.34)
  local copies, waits for them, and re-layouts: 256 us -> 6.54 us
  Pallas kernels: 0 us -> 117 us
  other arithmetic: 63.9 us -> 0 us
  starting transfers between devices: 53.3 us -> 0 us
  matrix products: 45.9 us -> 0 us
  waiting for transfers between devices: 43.3 us -> 0 us
  between operations: 13.8 us -> 0.09 us
  blocking collectives: 44 us -> 55.1 us
    gather x54 -> x0, local copies, waits for them, and re-layouts: 213 us -> none  [step(): picked = jnp.take(table, local, axis=1)]
    pallas_call x0 -> x3, Pallas kernels: none -> 117 us  [the longest x2 94 us: run_block(): pl.pallas_call(functools.partial(block_kernel, block), out_shape=jax.Shap...]
    dot_general x74 -> x0, matrix products: 45.9 us -> none  [the longest x54 28 us: step(): return total + jnp.dot(kernel, picked, preferred_element_type=jnp.float32)]
    all_to_all x2 -> x0, starting transfers between devices: 33 us -> none  [the longest x1 17.3 us: relayout(): lax.all_to_all(spots, 'seq', split_axis=0, concat_axis=0, tiled=True)]
    reduce_scatter x2 -> x0, waiting for transfers between devices: 25.2 us -> none  [run_block(): lax.psum_scatter(partial_value.astype(jnp.bfloat16), 'head', scatter_dime...]
    min x54 -> x0, other arithmetic: 22.4 us -> none  [step(): local = jnp.clip(index - offset, 0, table.shape[1] - 1)]
    ge x54 -> x0, other arithmetic: 22.2 us -> none  [step(): picked = jnp.where((index >= 0)[None, :], picked, jnp.zeros_like(picked))]
    ppermute x4 -> x0, starting transfers between devices: 20.3 us -> none  [the longest x2 13.2 us: extended(): before = lax.ppermute(last, axis, up)]
  transfers between devices with their start and end apart: 8 -> 0, of which waited for: 4 -> 0; matrix products, arithmetic and copies ran while one was open for 4% -> 0% of each run, Pallas kernels for 0% -> 0%
where the time goes in v1:
time: 179 us
  Pallas kernels  117 us (65%)
  blocking collectives  55.1 us (31%)
  local copies, waits for them, and re-layouts  6.54 us (4%)
    pallas_call x2, Pallas kernels, run_block(): pl.pallas_call(functools.partial(block_kernel, block), out_shape=jax.Shap...  94 us
    all_gather x1, blocking collectives, body(): lax.all_gather(hilbert_place.reshape(1, rows // 128, 128), 'seq', axis=0,...  55.1 us
    pallas_call x1, Pallas kernels, change_order(): pl.pallas_call(order_kernel, out_shape=jax.ShapeDtypeStruct((width, rows)...  22.7 us
    unnamed x22, local copies, waits for them, and re-layouts  6.54 us

profile of v1, /device:TPU:1, one launch (start us, length us, event | category | flops | bytes accessed | tf_op | source)
XLA Modules:
  0.0 178.5 jit_solution(14829224629119186686)
XLA Ops:
  0.0 0.0 copy-start.9
  0.0 1.0 copy.10.nbr
  1.0 0.0 copy-start
  1.0 1.5 copy-done
  2.5 0.0 copy-start.2
  2.5 0.9 copy-done.2
  3.4 0.0 copy-start.4
  3.4 0.8 copy-done.4
  4.3 0.0 copy-start.6
  4.3 0.9 copy-done.6
  5.2 0.0 copy-start.7
  5.2 0.7 copy-done.7
  5.9 0.0 copy-start.1
  5.9 0.0 copy-start.3
  5.9 50.4 %block0.1.x = bf16[64,1024]{1,0:T(8,128)(2,1)S(1)} custom-call(bf16[64,1024]{1,0:T(8,128)(2,1)S(1)} %copy-done.6, s32[2,27,1024]{2,1,0:T(8,128)S(1)} %copy.10.nbr, s32[2,1024]{1,0:T(2,128)S(1)} %copy-done.7, bf16[2,27,64,256]{3,2,1,0:T(8,128)(2,1)S(1)} %copy-done, bf16[2,3,64,256]{3,2,1,0:T(8,128)(2,1)S(1)} %copy-done.2, bf16[2,64,256]{2,1,0:T(8,128)(2,1)S(1)} %copy-done.4), custom_call_target="tpu_custom_call" | custom-call | tf_op jit(solution)/shard_map/block0/pallas_call | solution.py:268
  56.3 0.0 copy-done.9
  56.3 55.1 %all_gather.3 = s32[128,8,128]{2,1,0:T(8,128)S(1)} all-gather(s32[1,8,128]{2,1,0:T(8,128)S(1)} %bitcast.3), channel_id=1, replica_groups=mesh['seq'=128,'head'=4] {'seq'}, dimensions={0}, use_global_device_ids=true | all-gather | bytes 528384 | tf_op jit(solution)/shard_map/all_gather | solution.py:463
  111.4 22.7 %change_order.1.x = bf16[64,1024]{1,0:T(8,128)(2,1)S(1)} custom-call(bf16[64,1024]{1,0:T(8,128)(2,1)S(1)} %block0.1.x, s32[64,16,128]{2,1,0:T(8,128)S(1)} %bitcast.2), custom_call_target="tpu_custom_call" | custom-call | tf_op jit(solution)/shard_map/change_order/pallas_call | solution.py:433
  134.1 0.0 copy-done.1
  134.1 0.0 copy-done.3
  134.2 0.0 copy-done.5
  134.2 0.0 copy-done.8
  134.2 43.7 %block1.1 = bf16[64,1024]{1,0:T(8,128)(2,1)S(1)} custom-call(bf16[64,1024]{1,0:T(8,128)(2,1)S(1)} %change_order.1.x, s32[2,27,1024]{2,1,0:T(8,128)S(1)} %copy.10.nbr, s32[2,1024]{1,0:T(2,128)S(1)} %copy-done.8, bf16[2,27,64,256]{3,2,1,0:T(8,128)(2,1)S(1)} %copy-done.1, bf16[2,3,64,256]{3,2,1,0:T(8,128)(2,1)S(1)} %copy-done.3, bf16[2,64,256]{2,1,0:T(8,128)(2,1)S(1)} %copy-done.5), custom_call_target="tpu_custom_call" | custom-call | tf_op jit(solution)/shard_map/block1/pallas_call | solution.py:268
  177.9 0.7 copy.13
  (2 shorter events, 0.0 us)
Async XLA Ops:
  0.0 56.3 %copy-start.9 = (s32[1024]{0:T(1024)S(1)}, s32[1024]{0:T(1024)}, u32[]{:S(2)}) copy-start(s32[1024]{0:T(1024)} %param.13) | copy-start | bytes 12292
  1.0 1.5 copy-start
  2.5 0.9 copy-start.2
  3.4 0.8 copy-start.4
  4.3 0.9 copy-start.6
  5.2 0.7 copy-start.7
  5.9 128.3 %copy-start.1 = (bf16[2,27,64,256]{3,2,1,0:T(8,128)(2,1)S(1)}, bf16[2,27,64,256]{3,2,1,0:T(8,128)(2,1)}, u32[]{:S(2)}) copy-start(bf16[2,27,64,256]{3,2,1,0:T(8,128)(2,1)} %cw.3) | copy-start | bytes 5308420
  5.9 128.3 %copy-start.3 = (bf16[2,3,64,256]{3,2,1,0:T(8,128)(2,1)S(1)}, bf16[2,3,64,256]{3,2,1,0:T(8,128)(2,1)}, u32[]{:S(2)}) copy-start(bf16[2,3,64,256]{3,2,1,0:T(8,128)(2,1)} %aw.3) | copy-start | bytes 589828
  5.9 128.3 %copy-start.5 = (bf16[2,64,256]{2,1,0:T(8,128)(2,1)S(1)}, bf16[2,64,256]{2,1,0:T(8,128)(2,1)}, u32[]{:S(2)}) copy-start(bf16[2,64,256]{2,1,0:T(8,128)(2,1)} %pw.3) | copy-start | bytes 196612
  5.9 128.3 %copy-start.8 = (s32[2,1024]{1,0:T(2,128)S(1)}, s32[2,1024]{1,0:T(2,128)}, u32[]{:S(2)}) copy-start(s32[2,1024]{1,0:T(2,128)} %valid.3) | copy-start | bytes 24580

commit v2 on v1

--- a/solution.py
+++ b/solution.py
@@ -1,4 +1,5 @@
 import functools
+import math
 
 import jax
 import jax.numpy as jnp
@@ -28,7 +29,16 @@
     )
 
 
-def block_kernel(
+def block_kernel(block, x, nbr, valid, cw, aw, pw, *rest):
+    if block == 0:
+        place, out, places, *rest = rest
+        *rest, s6, r6, s7, r7, s8, r8 = rest
+    else:
+        out, *rest = rest
+    block_steps(block, x, nbr, valid, cw, aw, pw, out, *rest, (place, places, s6, r6, s7, r7, s8, r8) if block == 0 else None)
+
+
+def block_steps(
     block,
     x,
     nbr,
@@ -61,6 +71,7 @@
     r4,
     s5,
     r5,
+    spread_places,
 ):
     width, rows = out.shape
     heads = width // HD
@@ -84,17 +95,32 @@
         pl.semaphore_signal(barrier, inc=1, device_id=(s, other), device_id_type=MESH)
     for other in (before, after):
         pl.semaphore_signal(barrier, inc=1, device_id=(other, h), device_id_type=MESH)
+    greeted = groups + 1
+    if spread_places is not None:
+        place, places, s6, r6, s7, r7, s8, r8 = spread_places
+        side = places.shape[0]
+        core = lax.rem(s, 2)
+        zz = s // (2 * side)
+        yy = lax.rem(s // 2, side)
+        sibling = s + 1 - 2 * core
+        lines = [lax.rem(zz + d, side) for d in range(1, side)]
+        ranks = [lax.rem(yy + d, side) for d in range(1, side)]
+        for other in [(q * side + yy) * 2 + core for q in lines] + [(zz * side + q) * 2 + core for q in ranks]:
+            pl.semaphore_signal(barrier, inc=1, device_id=(other, h), device_id_type=MESH)
+        greeted += 2 * (side - 1)
     loads = [
         pltpu.make_async_copy(x, table.at[mine, pl.ds(REACH, rows)], local.at[0]),
-        pltpu.make_async_copy(nbr.at[block], nb, local.at[1]),
+        pltpu.make_async_copy(nbr, nb, local.at[1]),
         pltpu.make_async_copy(valid, vm, local.at[2]),
         pltpu.make_async_copy(cw.at[block], w, local.at[3]),
         pltpu.make_async_copy(aw.at[block], a, local.at[4]),
         pltpu.make_async_copy(pw.at[block], p.at[mine, :], local.at[5]),
     ]
+    if spread_places is not None:
+        loads.append(pltpu.make_async_copy(place, places.at[zz, yy, core], local.at[6]))
     for load in loads:
         load.start()
-    pl.semaphore_wait(barrier, groups + 1)
+    pl.semaphore_wait(barrier, greeted)
 
     pieces = ((0, REACH), (rows - REACH, REACH), (REACH, rows - 2 * REACH))
     sends = []
@@ -108,6 +134,12 @@
                 s,
                 other,
             )
+            copy.start()
+            sends.append(copy)
+
+    if spread_places is not None:
+        for d, other in enumerate(lines):
+            copy = remote(place, places.at[zz, yy, core], s6.at[d], r6.at[d], (other * side + yy) * 2 + core, h)
             copy.start()
             sends.append(copy)
 
@@ -153,45 +185,57 @@
     for load in loads[1:5]:
         load.wait()
     arrived(2)
-
-    step = 9
+    if spread_places is not None:
+        loads[6].wait()
+        for d in range(1, side):
+            theirs = places.at[lax.rem(zz + side - d, side), yy, core]
+            remote(place, theirs, s6.at[d - 1], r6.at[d - 1], s, h).wait_recv()
+        for d, other in enumerate(ranks):
+            column = places.at[:, yy, core]
+            copy = remote(column, column, s7.at[d], r7.at[d], (zz * side + other) * 2 + core, h)
+            copy.start()
+            sends.append(copy)
+
+    taps = w[...].reshape(TAPS * width, -1)
 
     def products(tile):
         points = table[:, tile * REACH : (tile + 1) * REACH]
-
-        def some(i, carry):
-            taps = w[pl.ds(i * step, step)].reshape(step * width, -1)
-            value = jnp.dot(taps, points, preferred_element_type=F32).astype(BF16)
-            y[pl.ds(i * step, step), tile] = value.reshape(step, width, REACH)
-            return carry
-
-        lax.fori_loop(0, TAPS // step, some, 0)
+        value = jnp.dot(taps, points, preferred_element_type=F32).astype(BF16)
+        y[:, tile] = value.reshape(TAPS, width, REACH)
 
     for tile in range(1, blocks + 1):
         products(tile)
+    if spread_places is not None:
+        for d in range(1, side):
+            theirs = places.at[:, lax.rem(yy + side - d, side), core]
+            remote(theirs, theirs, s7.at[d - 1], r7.at[d - 1], s, h).wait_recv()
+        column = places.at[:, :, core]
+        across = remote(column, column, s8.at[0], r8.at[0], sibling, h)
+        across.start()
+        sends.append(across)
     first.wait_recv()
     last.wait_recv()
     products(0)
     products(blocks + 1)
 
-    place = lax.broadcasted_iota(jnp.int32, (REACH, REACH), 0)
+    position = lax.broadcasted_iota(jnp.int32, (REACH, REACH), 0).astype(F32).astype(BF16)
+    one, zero = jnp.ones((), BF16), jnp.zeros((), BF16)
     for blk in range(blocks):
         cols = slice(blk * REACH, (blk + 1) * REACH)
         base = s * rows + (blk - 1) * REACH
-
-        def tap(t, total):
-            index = nb[pl.ds(t, 1), cols]
+        total = jnp.zeros((width, REACH), F32)
+        for t in range(TAPS):
+            index = nb[t, block : block + 1, cols]
             spot = index - base
             tile = jnp.where(index < 0, 3, spot >> 8)
-            pick = (place == (spot & (REACH - 1))).astype(F32).astype(BF16)
+            within = (spot & (REACH - 1)).astype(F32).astype(BF16)
+            pick = jnp.where(position == within, one, zero)
             terms = y[t, blk : blk + 3].reshape(3 * width, REACH)
             picked = jnp.dot(terms, pick, preferred_element_type=F32)
             term = jnp.where(tile == 0, picked[:width], 0.0)
             term = jnp.where(tile == 1, picked[width : 2 * width], term)
             term = jnp.where(tile == 2, picked[2 * width :], term)
-            return total + term
-
-        total = lax.fori_loop(0, TAPS, tap, jnp.zeros((width, REACH), F32), unroll=3)
+            total = total + term
         own = table[mine, REACH + blk * REACH : REACH + (blk + 1) * REACH].astype(F32)
         mix[mine, cols] = (own + total).astype(BF16)
         for d, other in enumerate(peers):
@@ -235,14 +279,12 @@
     pt[...] = p[...].astype(F32).T.astype(BF16)
 
     for hd in range(heads):
-        for blk in range(blocks):
-            cols = slice(blk * REACH, (blk + 1) * REACH)
-            scores = jnp.dot(kt[...], qm[hd, :, cols], preferred_element_type=F32)
-            top = jnp.max(scores, axis=0, keepdims=True)
-            probs = jnp.exp(scores - top).astype(BF16)
-            summed = jnp.dot(va[hd], probs, preferred_element_type=F32)
-            result = summed[:HD] / summed[HD : HD + 1]
-            ho[part(h, HD, hd * HD), cols] = result.astype(BF16)
+        scores = jnp.dot(kt[...], qm[hd], preferred_element_type=F32)
+        top = jnp.max(scores, axis=0, keepdims=True)
+        probs = jnp.exp((scores - top).astype(BF16))
+        summed = jnp.dot(va[hd], probs, preferred_element_type=F32)
+        result = summed[:HD] / summed[HD : HD + 1]
+        ho[part(h, HD, hd * HD), :] = result.astype(BF16)
         span = part(h, HD, hd * HD)
         for d, other in enumerate(peers):
             copy = remote(ho.at[span, :], ho.at[span, :], s4.at[hd, d], r4.at[hd, d], s, other)
@@ -254,25 +296,37 @@
             remote(theirs, theirs, s4.at[hd, d], r4.at[hd, d], s, other).wait_recv()
     update = jnp.dot(pt[mine, :], ho[...], preferred_element_type=F32)
     out[...] = (mix[mine, :].astype(F32) + update).astype(BF16)
+    if spread_places is not None:
+        theirs = places.at[:, :, 1 - core]
+        remote(theirs, theirs, s8.at[0], r8.at[0], sibling, h).wait_recv()
     for copy in sends:
         copy.wait_send()
 
 
-def run_block(block, groups, x, nbr, valid, cw, aw, pw):
+def run_block(block, groups, x, nbr, valid, cw, aw, pw, place=None, side=None):
     width, rows = x.shape
     channels = width * groups
     heads = width // HD
     blocks = rows // REACH
     others = groups - 1
     dma = pltpu.SemaphoreType.DMA
+    given = [x, nbr, valid, cw, aw, pw]
+    shapes = [jax.ShapeDtypeStruct((width, rows), BF16)]
+    specs = [pl.BlockSpec(memory_space=pltpu.VMEM)]
+    more = []
+    if place is not None:
+        given.append(place)
+        shapes.append(jax.ShapeDtypeStruct((side, side, 2) + place.shape, jnp.int32))
+        specs.append(pl.BlockSpec(memory_space=pl.ANY))
+        more = [dma((n,)) for n in (side - 1, side - 1, side - 1, side - 1, 1, 1)]
     return pl.pallas_call(
         functools.partial(block_kernel, block),
-        out_shape=jax.ShapeDtypeStruct((width, rows), BF16),
-        in_specs=[pl.BlockSpec(memory_space=pl.ANY)] * 6,
-        out_specs=pl.BlockSpec(memory_space=pltpu.VMEM),
+        out_shape=shapes,
+        in_specs=[pl.BlockSpec(memory_space=pl.ANY)] * len(given),
+        out_specs=specs,
         scratch_shapes=[
             pltpu.VMEM((channels, rows + 2 * REACH), BF16),
-            pltpu.VMEM((TAPS, rows), jnp.int32),
+            pltpu.VMEM((TAPS, 2, rows), jnp.int32),
             pltpu.VMEM((2, rows), jnp.int32),
             pltpu.VMEM((TAPS, width, channels), BF16),
             pltpu.VMEM((3, width, channels), BF16),
@@ -284,7 +338,7 @@
             pltpu.VMEM((heads, 2 * HD, rows), BF16),
             pltpu.VMEM((channels, rows), BF16),
             pltpu.VMEM((channels, channels), BF16),
-            dma((6,)),
+            dma((7,)),
             dma((3, others)),
             dma((3, others)),
             dma((2,)),
@@ -295,12 +349,13 @@
             dma((heads, others)),
             dma((others,)),
             dma((others,)),
+            *more,
         ],
         compiler_params=pltpu.CompilerParams(
-            collective_id=block, has_side_effects=True, vmem_limit_bytes=48 * 2**20
+            collective_id=block, has_side_effects=True, vmem_limit_bytes=60 * 2**20
         ),
         name=f"block{block}",
-    )(x, nbr, valid, cw, aw, pw)
+    )(*given)
 
 
 def order_kernel(x, places, out, pv, feats, tri, pick, going, come, land, flat, turned, local, s1, r1, s2, r2):
@@ -452,21 +507,18 @@
             dma((1,)),
         ],
         compiler_params=pltpu.CompilerParams(
-            collective_id=2, has_side_effects=True, vmem_limit_bytes=48 * 2**20
+            collective_id=2, has_side_effects=True, vmem_limit_bytes=60 * 2**20
         ),
         name="change_order",
     )(x, places)
 
 
-def body(groups, features, neighbours, valid, conv_weight, attn_weight, proj_weight, hilbert_place):
+def body(groups, side, features, neighbours, valid, conv_weight, attn_weight, proj_weight, hilbert_place):
     rows = hilbert_place.shape[0]
-    places = lax.all_gather(hilbert_place.reshape(1, rows // 128, 128), "seq", axis=0, tiled=True)
-    shards = places.shape[0]
-    places = places.reshape(shards // 2, rows // 64, 128)
-    rest = (neighbours, valid, conv_weight, attn_weight, proj_weight)
-    first = run_block(0, groups, features, *rest)
-    moved = change_order(first, places)
-    return run_block(1, groups, moved, *rest)
+    rest = (jnp.swapaxes(neighbours, 0, 1), valid, conv_weight, attn_weight, proj_weight)
+    first, places = run_block(0, groups, features, *rest, hilbert_place.reshape(rows // 128, 128), side)
+    moved = change_order(first, places.reshape(side * side, rows // 64, 128))
+    return run_block(1, groups, moved, *rest)[0]
 
 
 def solution(mesh):
@@ -481,7 +533,7 @@
     )
     out_specs = P("head", "seq")
     return jax.shard_map(
-        functools.partial(body, mesh.shape["head"]),
+        functools.partial(body, mesh.shape["head"], math.isqrt(mesh.shape["seq"] // 2)),
         mesh=mesh,
         in_specs=in_specs,
         out_specs=out_specs,

time: 179 us -> 111 us (0.62)
  blocking collectives: 55.1 us -> 0 us
  Pallas kernels: 117 us -> 108 us
  local copies, waits for them, and re-layouts: 6.54 us -> 1.57 us
    all_gather x1 -> x0, blocking collectives: 55.1 us -> none  [body(): lax.all_gather(hilbert_place.reshape(1, rows // 128, 128), 'seq', axis=0,...]
    pallas_call x2, Pallas kernels: 94 us -> 79.5 us  [run_block(): pl.pallas_call(functools.partial(block_kernel, block), out_shape=shapes,...]
    pallas_call x1, Pallas kernels: 22.7 us -> 28.6 us  [change_order(): pl.pallas_call(order_kernel, out_shape=jax.ShapeDtypeStruct((width, rows)...]
    unnamed x22 -> x1, local copies, waits for them, and re-layouts: 6.54 us -> 1.57 us
where the time goes in v2:
time: 111 us; the launch traced here: 110 us
  Pallas kernels  108 us (97%)
  local copies, waits for them, and re-layouts  1.57 us (1%)
    pallas_call x2, Pallas kernels, run_block(): pl.pallas_call(functools.partial(block_kernel, block), out_shape=shapes,...  79.5 us
    pallas_call x1, Pallas kernels, change_order(): pl.pallas_call(order_kernel, out_shape=jax.ShapeDtypeStruct((width, rows)...  28.6 us

profile of v2, /device:TPU:1, one launch (start us, length us, event | category | flops | bytes accessed | tf_op | source)
XLA Modules:
  0.0 109.7 jit_solution(4526133063153435969)
XLA Ops:
  0.0 48.1 %block0.1 = (bf16[64,1024]{1,0:T(8,128)(2,1)}, s32[8,8,2,8,128]{4,3,2,1,0:T(8,128)}) custom-call(bf16[64,1024]{1,0:T(8,128)(2,1)} %x.1, s32[27,2,1024]{2,1,0:T(2,128)} %bitcast.3, s32[2,1024]{1,0:T(2,128)} %valid.3, bf16[2,27,64,256]{3,2,1,0:T(8,128)(2,1)} %cw.3, bf16[2,3,64,256]{3,2,1,0:T(8,128)(2,1)} %aw.3, bf16[2,64,256]{2,1,0:T(8,128)(2,1)} %pw.3, ...), custom_call_target="tpu_custom_call" | custom-call | tf_op jit(solution)/shard_map/block0/pallas_call | solution.py:322
  48.1 28.6 %change_order.1.x = bf16[64,1024]{1,0:T(8,128)(2,1)} custom-call(bf16[64,1024]{1,0:T(8,128)(2,1)} %get-tuple-element.7.x, s32[64,16,128]{2,1,0:T(8,128)} %bitcast.5), custom_call_target="tpu_custom_call" | custom-call | tf_op jit(solution)/shard_map/change_order/pallas_call | solution.py:488
  76.7 31.4 %block1.1 = bf16[64,1024]{1,0:T(8,128)(2,1)} custom-call(bf16[64,1024]{1,0:T(8,128)(2,1)} %change_order.1.x, s32[27,2,1024]{2,1,0:T(2,128)} %bitcast.4, s32[2,1024]{1,0:T(2,128)} %valid.3, bf16[2,27,64,256]{3,2,1,0:T(8,128)(2,1)} %cw.3, bf16[2,3,64,256]{3,2,1,0:T(8,128)(2,1)} %aw.3, bf16[2,64,256]{2,1,0:T(8,128)(2,1)} %pw.3), custom_call_target="tpu_custom_call" | custom-call | tf_op jit(solution)/shard_map/block1/pallas_call | solution.py:322
  108.1 1.6 %copy.9 = bf16[64,1024]{1,0:T(8,128)(2,1)} copy(bf16[64,1024]{1,0:T(8,128)(2,1)} %block1.1) | data formatting | bytes 262144

commit v3 on v2

--- a/solution.py
+++ b/solution.py
@@ -81,8 +81,9 @@
     h = lax.axis_index("head")
     after = lax.rem(s + 1, shards)
     before = lax.rem(s + shards - 1, shards)
-    peers = [lax.rem(h + d, groups) for d in range(1, groups)]
-    froms = [lax.rem(h + groups - d, groups) for d in range(1, groups)]
+    right = lax.rem(h + 1, groups)
+    left = lax.rem(h + groups - 1, groups)
+    far = lax.rem(h + 2, groups)
     blocks = rows // REACH
 
     def part(index, size=width, extra=0):
@@ -91,11 +92,11 @@
     mine = part(h)
 
     barrier = pltpu.get_barrier_semaphore()
-    for other in peers:
+    for other in (right, left):
         pl.semaphore_signal(barrier, inc=1, device_id=(s, other), device_id_type=MESH)
     for other in (before, after):
         pl.semaphore_signal(barrier, inc=1, device_id=(other, h), device_id_type=MESH)
-    greeted = groups + 1
+    greeted = 4
     if spread_places is not None:
         place, places, s6, r6, s7, r7, s8, r8 = spread_places
         side = places.shape[0]
@@ -122,41 +123,50 @@
         load.start()
     pl.semaphore_wait(barrier, greeted)
 
-    pieces = ((0, REACH), (rows - REACH, REACH), (REACH, rows - 2 * REACH))
     sends = []
-    for j, (low, size) in enumerate(pieces):
-        for d, other in enumerate(peers):
-            copy = remote(
-                x.at[:, pl.ds(low, size)],
-                table.at[mine, pl.ds(REACH + low, size)],
-                s1.at[j, d],
-                r1.at[j, d],
-                s,
-                other,
-            )
+
+    def spread(source, piece, send, recv):
+        for i, other in enumerate((right, left)):
+            copy = remote(source, piece(h), send.at[i], recv.at[i], s, other)
             copy.start()
             sends.append(copy)
 
+    def forward(piece, send, recv):
+        for i, (origin, other) in enumerate(((left, right), (right, left))):
+            theirs = piece(origin)
+            remote(theirs, theirs, send.at[i], recv.at[i], s, other).wait_recv()
+            half = piece(origin, i)
+            copy = remote(half, half, send.at[2 + i], recv.at[2 + i], s, other)
+            copy.start()
+            sends.append(copy)
+
+    def finish(piece, send, recv):
+        for i in range(2):
+            half = piece(far, i)
+            remote(half, half, send.at[2 + i], recv.at[2 + i], s, right).wait_recv()
+
+    def strip(ref, cols):
+        def piece(index, half=None):
+            if half is None:
+                return ref.at[part(index), cols]
+            return ref.at[part(index, width // 2, half * (width // 2)), cols]
+
+        return piece
+
+    pieces = ((0, REACH), (rows - REACH, REACH), (REACH, rows - 2 * REACH))
+    inputs = [(strip(table, pl.ds(REACH + low, size)), s1.at[j], r1.at[j]) for j, (low, size) in enumerate(pieces)]
+    for (low, size), item in zip(pieces, inputs):
+        spread(x.at[:, pl.ds(low, size)], *item)
     if spread_places is not None:
         for d, other in enumerate(lines):
             copy = remote(place, places.at[zz, yy, core], s6.at[d], r6.at[d], (other * side + yy) * 2 + core, h)
             copy.start()
             sends.append(copy)
 
-    def arrived(j):
-        low, size = pieces[j]
-        for d, other in enumerate(froms):
-            remote(
-                x.at[:, pl.ds(low, size)],
-                table.at[part(other), pl.ds(REACH + low, size)],
-                s1.at[j, d],
-                r1.at[j, d],
-                s,
-                other,
-            ).wait_recv()
-
     loads[0].wait()
-    arrived(0)
+    forward(*inputs[0])
+    forward(*inputs[1])
+    finish(*inputs[0])
     first = remote(
         table.at[:, pl.ds(REACH, REACH)],
         table.at[:, pl.ds(REACH + rows, REACH)],
@@ -166,7 +176,7 @@
         h,
     )
     first.start()
-    arrived(1)
+    finish(*inputs[1])
     last = remote(
         table.at[:, pl.ds(rows, REACH)],
         table.at[:, pl.ds(0, REACH)],
@@ -177,14 +187,25 @@
     )
     last.start()
     sends += [first, last]
-    loads[5].wait()
-    for d, other in enumerate(peers):
-        copy = remote(p.at[mine, :], p.at[mine, :], s5.at[d], r5.at[d], s, other)
-        copy.start()
-        sends.append(copy)
     for load in loads[1:5]:
         load.wait()
-    arrived(2)
+
+    taps = w[...].reshape(TAPS * width, -1)
+
+    def products(tile):
+        points = table[:, tile * REACH : (tile + 1) * REACH]
+        value = jnp.dot(taps, points, preferred_element_type=F32).astype(BF16)
+        y[:, tile] = value.reshape(TAPS, width, REACH)
+
+    products(1)
+    forward(*inputs[2])
+    products(blocks)
+    finish(*inputs[2])
+    loads[5].wait()
+    whole = (strip(p, pl.ds(0, p.shape[1])), s5, r5)
+    spread(p.at[mine, :], *whole)
+    for tile in range(2, blocks):
+        products(tile)
     if spread_places is not None:
         loads[6].wait()
         for d in range(1, side):
@@ -195,24 +216,6 @@
             copy = remote(column, column, s7.at[d], r7.at[d], (zz * side + other) * 2 + core, h)
             copy.start()
             sends.append(copy)
-
-    taps = w[...].reshape(TAPS * width, -1)
-
-    def products(tile):
-        points = table[:, tile * REACH : (tile + 1) * REACH]
-        value = jnp.dot(taps, points, preferred_element_type=F32).astype(BF16)
-        y[:, tile] = value.reshape(TAPS, width, REACH)
-
-    for tile in range(1, blocks + 1):
-        products(tile)
-    if spread_places is not None:
-        for d in range(1, side):
-            theirs = places.at[:, lax.rem(yy + side - d, side), core]
-            remote(theirs, theirs, s7.at[d - 1], r7.at[d - 1], s, h).wait_recv()
-        column = places.at[:, :, core]
-        across = remote(column, column, s8.at[0], r8.at[0], sibling, h)
-        across.start()
-        sends.append(across)
     first.wait_recv()
     last.wait_recv()
     products(0)
@@ -220,6 +223,7 @@
 
     position = lax.broadcasted_iota(jnp.int32, (REACH, REACH), 0).astype(F32).astype(BF16)
     one, zero = jnp.ones((), BF16), jnp.zeros((), BF16)
+    mixes = [(strip(mix, pl.ds(blk * REACH, REACH)), s3.at[blk], r3.at[blk]) for blk in range(blocks)]
     for blk in range(blocks):
         cols = slice(blk * REACH, (blk + 1) * REACH)
         base = s * rows + (blk - 1) * REACH
@@ -238,10 +242,18 @@
             total = total + term
         own = table[mine, REACH + blk * REACH : REACH + (blk + 1) * REACH].astype(F32)
         mix[mine, cols] = (own + total).astype(BF16)
-        for d, other in enumerate(peers):
-            copy = remote(mix.at[mine, cols], mix.at[mine, cols], s3.at[blk, d], r3.at[blk, d], s, other)
-            copy.start()
-            sends.append(copy)
+        spread(mix.at[mine, cols], *mixes[blk])
+        if blk >= 2:
+            forward(*mixes[blk - 2])
+    forward(*whole)
+    if spread_places is not None:
+        for d in range(1, side):
+            theirs = places.at[:, lax.rem(yy + side - d, side), core]
+            remote(theirs, theirs, s7.at[d - 1], r7.at[d - 1], s, h).wait_recv()
+        column = places.at[:, :, core]
+        across = remote(column, column, s8.at[0], r8.at[0], sibling, h)
+        across.start()
+        sends.append(across)
 
     scale = 1.0 / HD**0.5
     bias = jnp.where(vm[block : block + 1, :] > 0, 0.0, -1e30)
@@ -253,13 +265,13 @@
     weights = a[...].reshape(3 * width, -1)
     for blk in range(blocks):
         cols = slice(blk * REACH, (blk + 1) * REACH)
-        for d, other in enumerate(froms):
-            theirs = mix.at[part(other), cols]
-            remote(theirs, theirs, s3.at[blk, d], r3.at[blk, d], s, other).wait_recv()
+        if blk + blocks - 2 < blocks:
+            forward(*mixes[blk + blocks - 2])
+        finish(*mixes[blk])
         values = mix[:, cols].astype(F32)
         centred = values - jnp.mean(values, axis=0, keepdims=True)
-        spread = jnp.mean(centred * centred, axis=0, keepdims=True)
-        normed = (centred * lax.rsqrt(spread + 1e-05)).astype(BF16)
+        variance = jnp.mean(centred * centred, axis=0, keepdims=True)
+        normed = (centred * lax.rsqrt(variance + 1e-05)).astype(BF16)
         qkv = jnp.dot(weights, normed, preferred_element_type=F32)
         query = (qkv[:width].astype(BF16).astype(F32) * scale).astype(BF16)
         value = qkv[2 * width :].astype(BF16)
@@ -273,11 +285,17 @@
         keys = jnp.concatenate([qkv[width : 2 * width], tail], axis=0)
         kt[cols, :] = keys.T.astype(BF16)
 
-    for d, other in enumerate(froms):
-        theirs = p.at[part(other), :]
-        remote(theirs, theirs, s5.at[d], r5.at[d], s, other).wait_recv()
+    finish(*whole)
     pt[...] = p[...].astype(F32).T.astype(BF16)
 
+    def lane(hd):
+        def piece(index, half=None):
+            cols = pl.ds(0, rows) if half is None else pl.ds(half * (rows // 2), rows // 2)
+            return ho.at[part(index, HD, hd * HD), cols]
+
+        return piece
+
+    results = [(lane(hd), s4.at[hd], r4.at[hd]) for hd in range(heads)]
     for hd in range(heads):
         scores = jnp.dot(kt[...], qm[hd], preferred_element_type=F32)
         top = jnp.max(scores, axis=0, keepdims=True)
@@ -285,15 +303,12 @@
         summed = jnp.dot(va[hd], probs, preferred_element_type=F32)
         result = summed[:HD] / summed[HD : HD + 1]
         ho[part(h, HD, hd * HD), :] = result.astype(BF16)
-        span = part(h, HD, hd * HD)
-        for d, other in enumerate(peers):
-            copy = remote(ho.at[span, :], ho.at[span, :], s4.at[hd, d], r4.at[hd, d], s, other)
-            copy.start()
-            sends.append(copy)
-    for hd in range(heads):
-        for d, other in enumerate(froms):
-            theirs = ho.at[part(other, HD, hd * HD), :]
-            remote(theirs, theirs, s4.at[hd, d], r4.at[hd, d], s, other).wait_recv()
+        spread(ho.at[part(h, HD, hd * HD), :], *results[hd])
+        if hd >= 1:
+            forward(*results[hd - 1])
+    forward(*results[heads - 1])
+    for item in results:
+        finish(*item)
     update = jnp.dot(pt[mine, :], ho[...], preferred_element_type=F32)
     out[...] = (mix[mine, :].astype(F32) + update).astype(BF16)
     if spread_places is not None:
@@ -308,7 +323,6 @@
     channels = width * groups
     heads = width // HD
     blocks = rows // REACH
-    others = groups - 1
     dma = pltpu.SemaphoreType.DMA
     given = [x, nbr, valid, cw, aw, pw]
     shapes = [jax.ShapeDtypeStruct((width, rows), BF16)]
@@ -339,16 +353,16 @@
             pltpu.VMEM((channels, rows), BF16),
             pltpu.VMEM((channels, channels), BF16),
             dma((7,)),
-            dma((3, others)),
-            dma((3, others)),
+            dma((3, 4)),
+            dma((3, 4)),
             dma((2,)),
             dma((2,)),
-            dma((blocks, others)),
-            dma((blocks, others)),
-            dma((heads, others)),
-            dma((heads, others)),
-            dma((others,)),
-            dma((others,)),
+            dma((blocks, 4)),
+            dma((blocks, 4)),
+            dma((heads, 4)),
+            dma((heads, 4)),
+            dma((4,)),
+            dma((4,)),
             *more,
         ],
         compiler_params=pltpu.CompilerParams(
@@ -358,7 +372,7 @@
     )(*given)
 
 
-def order_kernel(x, places, out, pv, feats, tri, pick, going, come, land, flat, turned, local, s1, r1, s2, r2):
+def order_kernel(x, places, out, pv, pl_own, feats, tri, pick, going, come, land, flat, found, turned, local, s1, r1, s2, r2):
     width, rows = x.shape
     chips = places.shape[0]
     lines = places.shape[1]
@@ -368,6 +382,7 @@
     core = lax.rem(s, 2)
     chip = s // 2
     sibling = s + 1 - 2 * core
+    bits = rows.bit_length() - 1
 
     barrier = pltpu.get_barrier_semaphore()
 
@@ -378,11 +393,13 @@
 
     pl.semaphore_signal(barrier, inc=1, device_id=(sibling, h), device_id_type=MESH)
     lax.fori_loop(1, chips, greet, 0)
-    load = pltpu.make_async_copy(places, pv, local.at[0])
-    load.start()
+    near = pltpu.make_async_copy(places.at[chip], pl_own, local.at[0])
+    near.start()
+    for line in range(lines):
+        pltpu.make_async_copy(places.at[:, line], pv.at[line], local.at[3]).start()
     keep = pltpu.make_async_copy(x, feats.at[core], local.at[1])
     keep.start()
-    load.wait()
+    near.wait()
     pl.semaphore_wait(barrier, chips)
     swap = remote(x, feats.at[core], s1.at[0], r1.at[0], sibling, h)
     swap.start()
@@ -395,15 +412,15 @@
     run = jnp.zeros((chips, 1), F32)
     slots = []
     for line in range(lines):
-        row = pv[chip, line : line + 1, :]
-        device = row // rows
+        row = pl_own[line : line + 1, :]
+        device = row >> bits
         mask = jnp.where(device == column * 2 + core, 1.0, 0.0)
         counts = jnp.dot(mask.astype(BF16), tri[...], preferred_element_type=F32) + run
         run = counts[:, lanes - 1 :]
         rank = (jnp.sum(mask * counts, axis=0, keepdims=True) - 1.0).astype(jnp.int32)
-        here = lax.rem(device, 2) == core
-        target = (device // 2) * CAP + (rank & (CAP - 1))
-        slots.append((jnp.where(here, target, -1), rank // CAP))
+        here = (device & 1) == core
+        target = (device >> 1) * CAP + (rank & (CAP - 1))
+        slots.append((jnp.where(here, target, -1), rank >> 4))
     targets = jnp.concatenate([t for t, _ in slots], axis=1)
     halves = jnp.concatenate([e for _, e in slots], axis=1)
     for e in range(2):
@@ -443,25 +460,39 @@
     stay = pltpu.make_async_copy(going.at[chip], come.at[chip], local.at[2])
     stay.start()
 
+    pltpu.make_async_copy(places.at[:, pl.ds(0, lines)], places.at[:, pl.ds(0, lines)], local.at[3]).wait()
     run = jnp.zeros((chips, 1), F32)
     for line in range(lines):
-        row = pv[:, line, :]
-        mask = jnp.where(row // rows == s, 1.0, 0.0)
+        row = pv[line]
+        mask = jnp.where((row >> bits) == s, 1.0, 0.0)
         counts = jnp.dot(mask.astype(BF16), tri[...], preferred_element_type=F32) + run
         run = counts[:, lanes - 1 :]
         land[line] = jnp.where(mask > 0, counts - 1.0, -1.0)
         flat[line] = ((row & (rows - 1)) + 1).astype(F32)
-    where = lax.broadcasted_iota(jnp.int32, (chips, rows), 1).astype(F32) + 1.0
-
-    def settle(k, carry):
-        found = jnp.zeros((chips, lanes), F32)
-        for line in range(lines):
-            found += jnp.where(land[line] == k.astype(F32), flat[line], 0.0)
-        spots = jnp.sum(found, axis=1, keepdims=True)
-        turned[pl.ds(pl.multiple_of(k * chips, 16), chips), :] = (spots == where).astype(F32).astype(BF16)
+    for low in range(0, chips, 8):
+        ranks = [land[line, low : low + 8, :] for line in range(lines)]
+        spots = [flat[line, low : low + 8, :] for line in range(lines)]
+
+        def settle(k, carry):
+            rank = k.astype(F32)
+            total = jnp.zeros((8, lanes), F32)
+            for line in range(lines):
+                total += jnp.where(ranks[line] == rank, spots[line], 0.0)
+            place = jnp.sum(total, axis=1, keepdims=True)
+            found[pl.ds(pl.multiple_of(k * chips + low, 8), 8), :] = jnp.broadcast_to(place, (8, lanes))
+            return carry
+
+        lax.fori_loop(0, 2 * CAP, settle, 0, unroll=8)
+    where = lax.broadcasted_iota(jnp.int32, (chips, lanes), 1).astype(F32) + 1.0
+
+    def turn(k, carry):
+        span = pl.ds(pl.multiple_of(k * chips, 16), chips)
+        spots = found[span, :]
+        for low in range(0, rows, lanes):
+            turned[span, low : low + lanes] = (spots == where + float(low)).astype(F32).astype(BF16)
         return carry
 
-    lax.fori_loop(0, 2 * CAP, settle, 0)
+    lax.fori_loop(0, 2 * CAP, turn, 0, unroll=2)
 
     stay.wait()
     many = pl.ds(0, chips - 1)
@@ -491,7 +522,8 @@
         in_specs=[pl.BlockSpec(memory_space=pl.ANY)] * 2,
         out_specs=pl.BlockSpec(memory_space=pltpu.VMEM),
         scratch_shapes=[
-            pltpu.VMEM((chips, lines, lanes), jnp.int32),
+            pltpu.VMEM((lines, chips, lanes), jnp.int32),
+            pltpu.VMEM((lines, lanes), jnp.int32),
             pltpu.VMEM((2, width, rows), BF16),
             pltpu.VMEM((lanes, lanes), BF16),
             pltpu.VMEM((2, 2 * rows), jnp.int32),
@@ -499,8 +531,9 @@
             pltpu.VMEM((chips, CAP, 2 * width), BF16),
             pltpu.VMEM((lines, chips, lanes), F32),
             pltpu.VMEM((lines, chips, lanes), F32),
+            pltpu.VMEM((2 * CAP * chips, lanes), F32),
             pltpu.VMEM((2 * CAP * chips, rows), BF16),
-            dma((3,)),
+            dma((4,)),
             dma((1,)),
             dma((1,)),
             dma((1,)),

time: 111 us -> 124 us (1.12)
  the two profiles are of different devices: /device:TPU:1 before, /device:TPU:2 now
where the time goes in v3:
time: 124 us
  Pallas kernels  122 us (98%)
  local copies, waits for them, and re-layouts  1.57 us (1%)
    pallas_call x2, Pallas kernels, run_block(): pl.pallas_call(functools.partial(block_kernel, block), out_shape=shapes,...  97.9 us
    pallas_call x1, Pallas kernels, change_order(): pl.pallas_call(order_kernel, out_shape=jax.ShapeDtypeStruct((width, rows)...  24.1 us

profile of v3, /device:TPU:2, one launch (start us, length us, event | category | flops | bytes accessed | tf_op | source)
XLA Modules:
  0.0 123.6 jit_solution(7873746403431850151)
XLA Ops:
  0.0 53.8 %block0.1 = (bf16[64,1024]{1,0:T(8,128)(2,1)}, s32[8,8,2,8,128]{4,3,2,1,0:T(8,128)}) custom-call(bf16[64,1024]{1,0:T(8,128)(2,1)} %x.1, s32[27,2,1024]{2,1,0:T(2,128)} %bitcast.3, s32[2,1024]{1,0:T(2,128)} %valid.3, bf16[2,27,64,256]{3,2,1,0:T(8,128)(2,1)} %cw.3, bf16[2,3,64,256]{3,2,1,0:T(8,128)(2,1)} %aw.3, bf16[2,64,256]{2,1,0:T(8,128)(2,1)} %pw.3, ...), custom_call_target="tpu_custom_call" | custom-call | tf_op jit(solution)/shard_map/block0/pallas_call | solution.py:336
  53.8 24.1 %change_order.1.x = bf16[64,1024]{1,0:T(8,128)(2,1)} custom-call(bf16[64,1024]{1,0:T(8,128)(2,1)} %get-tuple-element.7.x, s32[64,16,128]{2,1,0:T(8,128)} %bitcast.5), custom_call_target="tpu_custom_call" | custom-call | tf_op jit(solution)/shard_map/change_order/pallas_call | solution.py:519
  77.9 44.1 %block1.1 = bf16[64,1024]{1,0:T(8,128)(2,1)} custom-call(bf16[64,1024]{1,0:T(8,128)(2,1)} %change_order.1.x, s32[27,2,1024]{2,1,0:T(2,128)} %bitcast.4, s32[2,1024]{1,0:T(2,128)} %valid.3, bf16[2,27,64,256]{3,2,1,0:T(8,128)(2,1)} %cw.3, bf16[2,3,64,256]{3,2,1,0:T(8,128)(2,1)} %aw.3, bf16[2,64,256]{2,1,0:T(8,128)(2,1)} %pw.3), custom_call_target="tpu_custom_call" | custom-call | tf_op jit(solution)/shard_map/block1/pallas_call | solution.py:336
  122.0 1.6 %copy.9 = bf16[64,1024]{1,0:T(8,128)(2,1)} copy(bf16[64,1024]{1,0:T(8,128)(2,1)} %block1.1) | data formatting | bytes 262144

commit v4 on v0

v4 whole, which is shorter than its diff:
```python
import functools
import math

import jax
import jax.numpy as jnp
from jax import lax
from jax.experimental import pallas as pl
from jax.experimental.pallas import tpu as pltpu
from jax.sharding import PartitionSpec as P

HD = 16
REACH = 256
TAPS = 27
CAP = 16
LANES = 128
MESH = pl.DeviceIdType.MESH
BF16 = jnp.bfloat16
F32 = jnp.float32


def remote(src, dst, send, recv, s, h):
    return pltpu.make_async_remote_copy(
        src_ref=src,
        dst_ref=dst,
        send_sem=send,
        recv_sem=recv,
        device_id=(s, h),
        device_id_type=MESH,
    )


def kernel(
    x,
    nbr,
    valid,
    cw,
    aw,
    pw,
    place,
    out,
    tables,
    mixes,
    heads_out,
    nb,
    vm,
    w,
    a,
    p,
    pt,
    y,
    kt,
    qm,
    va,
    places,
    pv,
    feats,
    tri,
    pick,
    going,
    come,
    land,
    flat,
    found,
    turned,
    moved,
    local,
    s1,
    r1,
    s2,
    r2,
    s3,
    r3,
    s4,
    r4,
    s5,
    r5,
    s6,
    r6,
    s7,
    r7,
    s8,
    r8,
    s9,
    r9,
    s10,
    r10,
):
    width, rows = out.shape
    heads = width // HD
    groups = lax.axis_size("head")
    shards = lax.axis_size("seq")
    side = places.shape[0]
    chips = side * side
    lines = 2 * places.shape[3]
    blocks = rows // REACH
    bits = rows.bit_length() - 1
    s = lax.axis_index("seq")
    h = lax.axis_index("head")
    core = lax.rem(s, 2)
    chip = s // 2
    zz = chip // side
    yy = lax.rem(chip, side)
    sibling = s + 1 - 2 * core
    after = lax.rem(s + 1, shards)
    before = lax.rem(s + shards - 1, shards)
    peers = [lax.rem(h + d, groups) for d in range(1, groups)]
    froms = [lax.rem(h + groups - d, groups) for d in range(1, groups)]
    sends = []

    def part(index, size=width, extra=0):
        return pl.ds(pl.multiple_of(index * width + extra, 16), size)

    mine = part(h)

    def ship(copy):
        copy.start()
        sends.append(copy)

    barrier = pltpu.get_barrier_semaphore()

    def greet(i, carry):
        other = lax.rem(chip + i, chips) * 2 + core
        pl.semaphore_signal(barrier, inc=1, device_id=(other, h), device_id_type=MESH)
        return carry

    for other in peers:
        pl.semaphore_signal(barrier, inc=1, device_id=(s, other), device_id_type=MESH)
    for other in (before, after):
        pl.semaphore_signal(barrier, inc=1, device_id=(other, h), device_id_type=MESH)
    lax.fori_loop(1, chips, greet, 0)
    loads = [
        pltpu.make_async_copy(x, tables.at[0, mine, pl.ds(REACH, rows)], local.at[0]),
        pltpu.make_async_copy(cw, w, local.at[1]),
        pltpu.make_async_copy(nbr, nb, local.at[2]),
        pltpu.make_async_copy(valid, vm, local.at[3]),
        pltpu.make_async_copy(aw, a, local.at[4]),
        pltpu.make_async_copy(pw, p.at[:, mine, :], local.at[5]),
        pltpu.make_async_copy(place, places.at[zz, yy, core], local.at[6]),
    ]
    for load in loads:
        load.start()
    low = lax.broadcasted_iota(jnp.int32, (LANES, LANES), 0)
    high = lax.broadcasted_iota(jnp.int32, (LANES, LANES), 1)
    tri[...] = jnp.where(low <= high, 1.0, 0.0).astype(BF16)
    position = lax.broadcasted_iota(jnp.int32, (REACH, REACH), 0).astype(F32).astype(BF16)
    one, zero = jnp.ones((), BF16), jnp.zeros((), BF16)
    ones = jnp.where(lax.broadcasted_iota(jnp.int32, (HD, rows), 0) == 0, 1.0, 0.0).astype(BF16)
    qm[...] = jnp.zeros(qm.shape, BF16)
    for hd in range(heads):
        qm[hd, width : width + HD, :] = ones
        va[hd, HD:, :] = ones
    pl.semaphore_wait(barrier, chips - 1 + groups - 1 + 2)

    order = (0, blocks - 1, *range(1, blocks - 1))

    def gather_start(b, source):
        for j in order:
            for d, other in enumerate(peers):
                span = pl.ds(REACH + j * REACH, REACH)
                ship(
                    remote(
                        source.at[:, pl.ds(j * REACH, REACH)],
                        tables.at[b, mine, span],
                        s1.at[b, j, d],
                        r1.at[b, j, d],
                        s,
                        other,
                    )
                )

    def gather_wait(b, j):
        for d, other in enumerate(froms):
            theirs = tables.at[b, part(other), pl.ds(REACH + j * REACH, REACH)]
            remote(theirs, theirs, s1.at[b, j, d], r1.at[b, j, d], s, other).wait_recv()

    def places_along_z():
        for d in range(1, side):
            other = (lax.rem(zz + d, side) * side + yy) * 2 + core
            ship(remote(place, places.at[zz, yy, core], s6.at[d - 1], r6.at[d - 1], other, h))

    def places_along_y():
        loads[6].wait()
        for d in range(1, side):
            theirs = places.at[lax.rem(zz + side - d, side), yy, core]
            remote(theirs, theirs, s6.at[d - 1], r6.at[d - 1], s, h).wait_recv()
        for d in range(1, side):
            other = (zz * side + lax.rem(yy + d, side)) * 2 + core
            column = places.at[:, yy, core]
            ship(remote(column, column, s7.at[d - 1], r7.at[d - 1], other, h))

    def places_across():
        for d in range(1, side):
            theirs = places.at[:, lax.rem(yy + side - d, side), core]
            remote(theirs, theirs, s7.at[d - 1], r7.at[d - 1], s, h).wait_recv()
        column = places.at[:, :, core]
        ship(remote(column, column, s8.at[0], r8.at[0], sibling, h))

    def places_finish():
        theirs = places.at[:, :, 1 - core]
        remote(theirs, theirs, s8.at[0], r8.at[0], sibling, h).wait_recv()
        for line in range(lines):
            pltpu.make_async_copy(
                places.at[:, :, line // (lines // 2), line % (lines // 2)], pv.at[line], local.at[7]
            ).start()

    def weights_start():
        loads[5].wait()
        for d, other in enumerate(peers):
            ship(remote(p.at[:, mine, :], p.at[:, mine, :], s5.at[d], r5.at[d], s, other))

    def weights_finish():
        for d, other in enumerate(froms):
            theirs = p.at[:, part(other), :]
            remote(theirs, theirs, s5.at[d], r5.at[d], s, other).wait_recv()
        for b in range(2):
            pt[b] = p[b].astype(F32).T.astype(BF16)

    def run_block(b):
        table = tables.at[b]
        mix = mixes.at[b]
        ho = heads_out.at[b]
        gather_wait(b, 0)
        first = remote(
            table.at[:, pl.ds(REACH, REACH)],
            table.at[:, pl.ds(REACH + rows, REACH)],
            s2.at[b, 0],
            r2.at[b, 0],
            before,
            h,
        )
        ship(first)
        gather_wait(b, blocks - 1)
        last = remote(
            table.at[:, pl.ds(rows, REACH)],
            table.at[:, pl.ds(0, REACH)],
            s2.at[b, 1],
            r2.at[b, 1],
            after,
            h,
        )
        ship(last)
        if b == 0:
            for load in loads[1:5]:
                load.wait()
        taps = w[b].reshape(TAPS * width, -1)

        def products(tile):
            points = table[:, tile * REACH : (tile + 1) * REACH]
            value = jnp.dot(taps, points, preferred_element_type=F32).astype(BF16)
            y[:, tile] = value.reshape(TAPS, width, REACH)

        def conv(blk):
            cols = slice(blk * REACH, (blk + 1) * REACH)
            base = s * rows + (blk - 1) * REACH
            total = jnp.zeros((width, REACH), F32)
            for t in range(TAPS):
                index = nb[t, b : b + 1, cols]
                spot = index - base
                tile = jnp.where(index < 0, 3, spot >> 8)
                within = (spot & (REACH - 1)).astype(F32).astype(BF16)
                chosen = jnp.where(position == within, one, zero)
                terms = y[t, blk : blk + 3].reshape(3 * width, REACH)
                picked = jnp.dot(terms, chosen, preferred_element_type=F32)
                term = jnp.where(tile == 0, picked[:width], 0.0)
                term = jnp.where(tile == 1, picked[width : 2 * width], term)
                term = jnp.where(tile == 2, picked[2 * width :], term)
                total = total + term
            own = table[mine, REACH + blk * REACH : REACH + (blk + 1) * REACH].astype(F32)
            mix[mine, cols] = (own + total).astype(BF16)
            for d, other in enumerate(peers):
                ship(remote(mix.at[mine, cols], mix.at[mine, cols], s3.at[b, blk, d], r3.at[b, blk, d], s, other))

        products(1)
        products(blocks)
        for tile in range(2, blocks):
            gather_wait(b, tile - 1)
            products(tile)
        for blk in range(1, blocks - 1):
            conv(blk)
        if b == 0:
            places_along_y()
        last.wait_recv()
        products(0)
        conv(0)
        first.wait_recv()
        products(blocks + 1)
        conv(blocks - 1)
        if b == 0:
            weights_start()
            places_across()

        scale = 1.0 / HD**0.5
        bias = jnp.where(vm[b : b + 1, :] > 0, 0.0, -1e30)
        weights = a[b].reshape(3 * width, -1)
        for blk in (*range(1, blocks - 1), 0, blocks - 1):
            cols = slice(blk * REACH, (blk + 1) * REACH)
            for d, other in enumerate(froms):
                theirs = mix.at[part(other), cols]
                remote(theirs, theirs, s3.at[b, blk, d], r3.at[b, blk, d], s, other).wait_recv()
            values = mix[:, cols].astype(F32)
            centred = values - jnp.mean(values, axis=0, keepdims=True)
            variance = jnp.mean(centred * centred, axis=0, keepdims=True)
            normed = (centred * lax.rsqrt(variance + 1e-05)).astype(BF16)
            qkv = jnp.dot(weights, normed, preferred_element_type=F32)
            query = (qkv[:width].astype(BF16).astype(F32) * scale).astype(BF16)
            value = qkv[2 * width :].astype(BF16)
            for hd in range(heads):
                span = slice(hd * HD, (hd + 1) * HD)
                qm[hd, span, cols] = query[span]
                va[hd, :HD, cols] = value[span]
            tail = jnp.where(
                lax.broadcasted_iota(jnp.int32, (width, REACH), 0) == 0, bias[:, cols], 0.0
            )
            keys = jnp.concatenate([qkv[width : 2 * width], tail], axis=0)
            kt[cols, :] = keys.T.astype(BF16)

        for hd in range(heads):
            scores = jnp.dot(kt[...], qm[hd], preferred_element_type=F32)
            top = jnp.max(scores, axis=0, keepdims=True)
            probs = jnp.exp((scores - top).astype(BF16))
            summed = jnp.dot(va[hd], probs, preferred_element_type=F32)
            result = summed[:HD] / summed[HD : HD + 1]
            span = part(h, HD, hd * HD)
            ho[span, :] = result.astype(BF16)
            for d, other in enumerate(peers):
                ship(remote(ho.at[span, :], ho.at[span, :], s4.at[b, hd, d], r4.at[b, hd, d], s, other))

    def project(b):
        mix = mixes.at[b]
        ho = heads_out.at[b]
        for hd in range(heads):
            for d, other in enumerate(froms):
                theirs = ho.at[part(other, HD, hd * HD), :]
                remote(theirs, theirs, s4.at[b, hd, d], r4.at[b, hd, d], s, other).wait_recv()
        update = jnp.dot(pt[b, mine, :], ho[...], preferred_element_type=F32)
        return (mix[mine, :].astype(F32) + update).astype(BF16)

    gather_start(0, x)
    places_along_z()
    loads[0].wait()
    run_block(0)

    weights_finish()
    places_finish()
    column = lax.broadcasted_iota(jnp.int32, (chips, LANES), 0)
    run = jnp.zeros((chips, 1), F32)
    slots = []
    for line in range(lines):
        half = lines // 2
        row = places[zz, yy, line // half, line % half : line % half + 1, :]
        device = row >> bits
        mask = jnp.where(device == column * 2 + core, 1.0, 0.0)
        counts = jnp.dot(mask.astype(BF16), tri[...], preferred_element_type=F32) + run
        run = counts[:, LANES - 1 :]
        rank = (jnp.sum(mask * counts, axis=0, keepdims=True) - 1.0).astype(jnp.int32)
        here = (device & 1) == core
        target = (device >> 1) * CAP + (rank & (CAP - 1))
        slots.append((jnp.where(here, target, -1), rank >> 4))
    targets = jnp.concatenate([t for t, _ in slots], axis=1)
    halves = jnp.concatenate([e for _, e in slots], axis=1)
    for e in range(2):
        pick[e : e + 1, :] = jnp.where(halves == e, targets, -1)

    feats[core] = project(0)
    swap = remote(feats.at[core], feats.at[core], s9.at[0], r9.at[0], sibling, h)
    ship(swap)
    theirs = feats.at[1 - core]
    remote(theirs, theirs, s9.at[0], r9.at[0], sibling, h).wait_recv()
    points = jnp.concatenate([feats[0], feats[1]], axis=1)
    batch = 16
    strip = batch * CAP
    strips = chips // batch
    own = chip // batch
    spot = lax.broadcasted_iota(jnp.int32, (strip, 2 * rows), 0)
    nt = (((1,), (1,)), ((), ()))

    def sort(i, carry):
        which = lax.rem(own + i, strips)
        sides = []
        for e in range(2):
            onehot = (spot + which * strip == pick[e : e + 1, :]).astype(F32).astype(BF16)
            sides.append(lax.dot_general(onehot, points, nt, preferred_element_type=F32))
        both = jnp.concatenate(sides, axis=1).astype(BF16)
        going[pl.ds(which * batch, batch)] = both.reshape(batch, CAP, 2 * width)

        def send(j, c):
            other = which * batch + lax.rem(chip + j, batch)

            @pl.when(other != chip)
            def _():
                remote(going.at[other], come.at[chip], s10.at[0], r10.at[0], other * 2 + core, h).start()

            return c

        lax.fori_loop(0, batch, send, 0)
        return carry

    lax.fori_loop(0, strips, sort, 0)
    stay = pltpu.make_async_copy(going.at[chip], come.at[chip], local.at[8])
    stay.start()

    pltpu.make_async_copy(pv, pv, local.at[7]).wait()
    run = jnp.zeros((chips, 1), F32)
    for line in range(lines):
        row = pv[line].reshape(chips, LANES)
        mask = jnp.where((row >> bits) == s, 1.0, 0.0)
        counts = jnp.dot(mask.astype(BF16), tri[...], preferred_element_type=F32) + run
        run = counts[:, LANES - 1 :]
        land[line] = jnp.where(mask > 0, counts - 1.0, -1.0)
        flat[line] = ((row & (rows - 1)) + 1).astype(F32)
    for start in range(0, chips, 8):
        ranks = [land[line, start : start + 8, :] for line in range(lines)]
        spots = [flat[line, start : start + 8, :] for line in range(lines)]

        def settle(k, carry):
            rank = k.astype(F32)
            total = jnp.zeros((8, LANES), F32)
            for line in range(lines):
                total += jnp.where(ranks[line] == rank, spots[line], 0.0)
            where = jnp.sum(total, axis=1, keepdims=True)
            found[pl.ds(pl.multiple_of(k * chips + start, 8), 8), :] = jnp.broadcast_to(where, (8, LANES))
            return carry

        lax.fori_loop(0, 2 * CAP, settle, 0, unroll=8)
    lane = lax.broadcasted_iota(jnp.int32, (chips, LANES), 1).astype(F32) + 1.0

    def turn(k, carry):
        span = pl.ds(pl.multiple_of(k * chips, 16), chips)
        spots = found[span, :]
        for start in range(0, rows, LANES):
            turned[span, start : start + LANES] = (spots == lane + float(start)).astype(F32).astype(BF16)
        return carry

    lax.fori_loop(0, 2 * CAP, turn, 0, unroll=2)

    stay.wait()
    many = pl.ds(0, chips - 1)
    every = remote(going.at[many], come.at[many], s10.at[0], r10.at[0], sibling, h)
    every.wait_recv()
    arrived = come[...].astype(F32)
    parts = []
    for k in range(0, CAP, 2):
        two = jnp.concatenate([arrived[:, k, :], arrived[:, k + 1, :]], axis=0)
        parts.append(two.T.astype(BF16))
    packed = jnp.concatenate(parts, axis=1)
    half = CAP * chips
    total = jnp.dot(packed[:width], turned[:half, :], preferred_element_type=F32)
    total += jnp.dot(packed[width:], turned[half:, :], preferred_element_type=F32)
    moved[...] = total.astype(BF16)
    gather_start(1, moved)
    tables[1, mine, REACH : REACH + rows] = moved[...]
    run_block(1)
    out[...] = project(1)
    for copy in sends:
        copy.wait_send()
    every.wait_send()


def body(groups, side, features, neighbours, valid, conv_weight, attn_weight, proj_weight, hilbert_place):
    width, rows = features.shape
    channels = width * groups
    heads = width // HD
    blocks = rows // REACH
    chips = side * side
    lines = 2 * rows // LANES
    others = groups - 1
    dma = pltpu.SemaphoreType.DMA
    vmem = pltpu.VMEM
    pairs = [(2, blocks, others), (2, 2), (2, blocks, others), (2, heads, others), (others,)]
    pairs += [(side - 1,), (side - 1,), (1,), (1,), (1,)]
    return pl.pallas_call(
        kernel,
        out_shape=jax.ShapeDtypeStruct((width, rows), BF16),
        in_specs=[pl.BlockSpec(memory_space=pl.ANY)] * 7,
        out_specs=pl.BlockSpec(memory_space=pltpu.VMEM),
        scratch_shapes=[
            vmem((2, channels, rows + 2 * REACH), BF16),
            vmem((2, channels, rows), BF16),
            vmem((2, channels, rows), BF16),
            vmem((TAPS, 2, rows), jnp.int32),
            vmem((2, rows), jnp.int32),
            vmem((2, TAPS, width, channels), BF16),
            vmem((2, 3, width, channels), BF16),
            vmem((2, channels, channels), BF16),
            vmem((2, channels, channels), BF16),
            vmem((TAPS, blocks + 2, width, REACH), BF16),
            vmem((rows, 2 * width), BF16),
            vmem((heads, 2 * width, rows), BF16),
            vmem((heads, 2 * HD, rows), BF16),
            vmem((side, side, 2, rows // LANES, LANES), jnp.int32),
            vmem((lines, side, side, LANES), jnp.int32),
            vmem((2, width, rows), BF16),
            vmem((LANES, LANES), BF16),
            vmem((2, 2 * rows), jnp.int32),
            vmem((chips, CAP, 2 * width), BF16),
            vmem((chips, CAP, 2 * width), BF16),
            vmem((lines, chips, LANES), F32),
            vmem((lines, chips, LANES), F32),
            vmem((2 * CAP * chips, LANES), F32),
            vmem((2 * CAP * chips, rows), BF16),
            vmem((width, rows), BF16),
            dma((9,)),
            *[dma(shape) for shape in pairs for _ in range(2)],
        ],
        compiler_params=pltpu.CompilerParams(
            collective_id=0, has_side_effects=True, vmem_limit_bytes=60 * 2**20
        ),
        name="blocks",
    )(
        features,
        jnp.swapaxes(neighbours, 0, 1),
        valid,
        conv_weight,
        attn_weight,
        proj_weight,
        hilbert_place.reshape(rows // LANES, LANES),
    )


def solution(mesh):
    in_specs = (
        P("head", "seq"),
        P(None, None, "seq"),
        P(None, "seq"),
        P(None, None, "head", None),
        P(None, None, "head", None),
        P(None, "head", None),
        P("seq"),
    )
    return jax.shard_map(
        functools.partial(body, mesh.shape["head"], math.isqrt(mesh.shape["seq"] // 2)),
        mesh=mesh,
        in_specs=in_specs,
        out_specs=P("head", "seq"),
        check_vma=False,
    )
```

time: 527 us -> 93.5 us (0.18)
  local copies, waits for them, and re-layouts: 256 us -> 1.57 us
  Pallas kernels: 0 us -> 91.8 us
  other arithmetic: 63.9 us -> 0 us
  starting transfers between devices: 53.3 us -> 0 us
  matrix products: 45.9 us -> 0 us
  blocking collectives: 44 us -> 0 us
  waiting for transfers between devices: 43.3 us -> 0 us
  between operations: 13.8 us -> 0.01 us
    gather x54 -> x0, local copies, waits for them, and re-layouts: 213 us -> none  [step(): picked = jnp.take(table, local, axis=1)]
    pallas_call x0 -> x1, Pallas kernels: none -> 91.8 us  [body(): pl.pallas_call(kernel, out_shape=jax.ShapeDtypeStruct((width, rows), BF16...]
    dot_general x74 -> x0, matrix products: 45.9 us -> none  [the longest x54 28 us: step(): return total + jnp.dot(kernel, picked, preferred_element_type=jnp.float32)]
    all_gather x4 -> x0, blocking collectives: 44 us -> none  [the longest x2 22.7 us: run_block(): whole = lax.all_gather(mixed, 'head', axis=0, tiled=True)]
    all_to_all x2 -> x0, starting transfers between devices: 33 us -> none  [the longest x1 17.3 us: relayout(): lax.all_to_all(spots, 'seq', split_axis=0, concat_axis=0, tiled=True)]
    reduce_scatter x2 -> x0, waiting for transfers between devices: 25.2 us -> none  [run_block(): lax.psum_scatter(partial_value.astype(jnp.bfloat16), 'head', scatter_dime...]
    min x54 -> x0, other arithmetic: 22.4 us -> none  [step(): local = jnp.clip(index - offset, 0, table.shape[1] - 1)]
    ge x54 -> x0, other arithmetic: 22.2 us -> none  [step(): picked = jnp.where((index >= 0)[None, :], picked, jnp.zeros_like(picked))]
  transfers between devices with their start and end apart: 8 -> 0, of which waited for: 4 -> 0; matrix products, arithmetic and copies ran while one was open for 4% -> 0% of each run, Pallas kernels for 0% -> 0%
where the time goes in v4:
time: 93.5 us; the launch traced here: 93.4 us
  Pallas kernels  91.8 us (98%)
  local copies, waits for them, and re-layouts  1.57 us (2%)
    pallas_call x1, Pallas kernels, body(): pl.pallas_call(kernel, out_shape=jax.ShapeDtypeStruct((width, rows), BF16...  91.8 us

profile of v4, /device:TPU:1, one launch (start us, length us, event | category | flops | bytes accessed | tf_op | source)
XLA Modules:
  0.0 93.4 jit_solution(4540175990393843266)
XLA Ops:
  0.0 91.8 %blocks.1 = bf16[64,1024]{1,0:T(8,128)(2,1)} custom-call(bf16[64,1024]{1,0:T(8,128)(2,1)} %x.1, s32[27,2,1024]{2,1,0:T(2,128)} %bitcast.2, s32[2,1024]{1,0:T(2,128)} %valid.1, bf16[2,27,64,256]{3,2,1,0:T(8,128)(2,1)} %cw.1, bf16[2,3,64,256]{3,2,1,0:T(8,128)(2,1)} %aw.1, bf16[2,64,256]{2,1,0:T(8,128)(2,1)} %pw.1, s32[8,128]{1,0:T(8,128)} %bitcast.3), custom_call_target="tpu_custom_call" | custom-call | tf_op jit(solution)/shard_map/blocks/pallas_call | solution.py:471
  91.8 1.6 %copy.9 = bf16[64,1024]{1,0:T(8,128)(2,1)} copy(bf16[64,1024]{1,0:T(8,128)(2,1)} %blocks.1) | data formatting | bytes 262144

commit v5 on v4

--- a/solution.py
+++ b/solution.py
@@ -46,6 +46,8 @@
     w,
     a,
     p,
+    pq,
+    pall,
     pt,
     y,
     kt,
@@ -55,7 +57,8 @@
     pv,
     feats,
     tri,
-    pick,
+    onehot,
+    partial,
     going,
     come,
     land,
@@ -134,7 +137,7 @@
         pltpu.make_async_copy(nbr, nb, local.at[2]),
         pltpu.make_async_copy(valid, vm, local.at[3]),
         pltpu.make_async_copy(aw, a, local.at[4]),
-        pltpu.make_async_copy(pw, p.at[:, mine, :], local.at[5]),
+        pltpu.make_async_copy(pw, p, local.at[5]),
         pltpu.make_async_copy(place, places.at[zz, yy, core], local.at[6]),
     ]
     for load in loads:
@@ -153,20 +156,19 @@
 
     order = (0, blocks - 1, *range(1, blocks - 1))
 
-    def gather_start(b, source):
-        for j in order:
-            for d, other in enumerate(peers):
-                span = pl.ds(REACH + j * REACH, REACH)
-                ship(
-                    remote(
-                        source.at[:, pl.ds(j * REACH, REACH)],
-                        tables.at[b, mine, span],
-                        s1.at[b, j, d],
-                        r1.at[b, j, d],
-                        s,
-                        other,
-                    )
+    def gather_piece(b, source, j):
+        for d, other in enumerate(peers):
+            span = pl.ds(REACH + j * REACH, REACH)
+            ship(
+                remote(
+                    source.at[:, pl.ds(j * REACH, REACH)],
+                    tables.at[b, mine, span],
+                    s1.at[b, j, d],
+                    r1.at[b, j, d],
+                    s,
+                    other,
                 )
+            )
 
     def gather_wait(b, j):
         for d, other in enumerate(froms):
@@ -205,15 +207,49 @@
 
     def weights_start():
         loads[5].wait()
+        both = jnp.concatenate([p[0], p[1]], axis=0).astype(F32)
+        pq[...] = both.T.astype(BF16)
         for d, other in enumerate(peers):
-            ship(remote(p.at[:, mine, :], p.at[:, mine, :], s5.at[d], r5.at[d], s, other))
+            ship(remote(pq.at[part(other), :], pall.at[h], s5.at[d], r5.at[d], s, other))
+        pall[h] = pq[mine, :]
 
     def weights_finish():
         for d, other in enumerate(froms):
-            theirs = p.at[:, part(other), :]
-            remote(theirs, theirs, s5.at[d], r5.at[d], s, other).wait_recv()
+            remote(pall.at[other], pall.at[other], s5.at[d], r5.at[d], s, other).wait_recv()
         for b in range(2):
-            pt[b] = p[b].astype(F32).T.astype(BF16)
+            span = slice(b * width, (b + 1) * width)
+            pt[b] = jnp.concatenate([pall[g, :, span].astype(F32) for g in range(groups)], axis=1).astype(BF16)
+
+    batch = 16
+    strip = batch * CAP
+    strips = chips // batch
+
+    def prepare():
+        weights_finish()
+        places_finish()
+        column = lax.broadcasted_iota(jnp.int32, (chips, LANES), 0)
+        run = jnp.zeros((chips, 1), F32)
+        half = lines // 2
+        slots = []
+        for line in range(lines):
+            row = places[zz, yy, line // half, line % half : line % half + 1, :]
+            device = row >> bits
+            mask = jnp.where(device == column * 2 + core, 1.0, 0.0)
+            counts = jnp.dot(mask.astype(BF16), tri[...], preferred_element_type=F32) + run
+            run = counts[:, LANES - 1 :]
+            rank = (jnp.sum(mask * counts, axis=0, keepdims=True) - 1.0).astype(jnp.int32)
+            here = (device & 1) == core
+            target = (device >> 1) * CAP + (rank & (CAP - 1))
+            slots.append((jnp.where(here, target, -1), rank >> 4))
+        spot = lax.broadcasted_iota(jnp.int32, (strip, rows), 0)
+        for c in range(2):
+            targets = jnp.concatenate([t for t, _ in slots[c * half : (c + 1) * half]], axis=1)
+            halves = jnp.concatenate([e for _, e in slots[c * half : (c + 1) * half]], axis=1)
+            for e in range(2):
+                wanted = jnp.where(halves == e, targets, -1)
+                for i in range(strips):
+                    rows_of = slice(i * strip, (i + 1) * strip)
+                    onehot[e, c, rows_of, :] = (spot == wanted - i * strip).astype(F32).astype(BF16)
 
     def run_block(b):
         table = tables.at[b]
@@ -240,6 +276,7 @@
         )
         ship(last)
         if b == 0:
+            places_along_y()
             for load in loads[1:5]:
                 load.wait()
         taps = w[b].reshape(TAPS * width, -1)
@@ -278,7 +315,7 @@
         for blk in range(1, blocks - 1):
             conv(blk)
         if b == 0:
-            places_along_y()
+            places_across()
         last.wait_recv()
         products(0)
         conv(0)
@@ -286,8 +323,7 @@
         products(blocks + 1)
         conv(blocks - 1)
         if b == 0:
-            weights_start()
-            places_across()
+            prepare()
 
         scale = 1.0 / HD**0.5
         bias = jnp.where(vm[b : b + 1, :] > 0, 0.0, -1e30)
@@ -314,10 +350,16 @@
             keys = jnp.concatenate([qkv[width : 2 * width], tail], axis=0)
             kt[cols, :] = keys.T.astype(BF16)
 
+        def score(hd):
+            return jnp.dot(kt[...], qm[hd], preferred_element_type=F32)
+
+        upcoming = score(0)
         for hd in range(heads):
-            scores = jnp.dot(kt[...], qm[hd], preferred_element_type=F32)
+            scores = upcoming
+            if hd + 1 < heads:
+                upcoming = score(hd + 1)
             top = jnp.max(scores, axis=0, keepdims=True)
-            probs = jnp.exp((scores - top).astype(BF16))
+            probs = jnp.exp(scores - top).astype(BF16)
             summed = jnp.dot(va[hd], probs, preferred_element_type=F32)
             result = summed[:HD] / summed[HD : HD + 1]
             span = part(h, HD, hd * HD)
@@ -332,55 +374,43 @@
             for d, other in enumerate(froms):
                 theirs = ho.at[part(other, HD, hd * HD), :]
                 remote(theirs, theirs, s4.at[b, hd, d], r4.at[b, hd, d], s, other).wait_recv()
-        update = jnp.dot(pt[b, mine, :], ho[...], preferred_element_type=F32)
+        update = jnp.dot(pt[b], ho[...], preferred_element_type=F32)
         return (mix[mine, :].astype(F32) + update).astype(BF16)
 
-    gather_start(0, x)
+    for j in order:
+        gather_piece(0, x, j)
     places_along_z()
+    weights_start()
     loads[0].wait()
     run_block(0)
-
-    weights_finish()
-    places_finish()
-    column = lax.broadcasted_iota(jnp.int32, (chips, LANES), 0)
-    run = jnp.zeros((chips, 1), F32)
-    slots = []
-    for line in range(lines):
-        half = lines // 2
-        row = places[zz, yy, line // half, line % half : line % half + 1, :]
-        device = row >> bits
-        mask = jnp.where(device == column * 2 + core, 1.0, 0.0)
-        counts = jnp.dot(mask.astype(BF16), tri[...], preferred_element_type=F32) + run
-        run = counts[:, LANES - 1 :]
-        rank = (jnp.sum(mask * counts, axis=0, keepdims=True) - 1.0).astype(jnp.int32)
-        here = (device & 1) == core
-        target = (device >> 1) * CAP + (rank & (CAP - 1))
-        slots.append((jnp.where(here, target, -1), rank >> 4))
-    targets = jnp.concatenate([t for t, _ in slots], axis=1)
-    halves = jnp.concatenate([e for _, e in slots], axis=1)
-    for e in range(2):
-        pick[e : e + 1, :] = jnp.where(halves == e, targets, -1)
 
     feats[core] = project(0)
     swap = remote(feats.at[core], feats.at[core], s9.at[0], r9.at[0], sibling, h)
     ship(swap)
+    own = chip // batch
+    nt = (((1,), (1,)), ((), ()))
+
+    def sorted_part(c, which):
+        span = pl.ds(pl.multiple_of(which * strip, strip), strip)
+        points = feats[c]
+        sides = [
+            lax.dot_general(onehot[e, c, span, :], points, nt, preferred_element_type=F32) for e in range(2)
+        ]
+        return span, jnp.concatenate(sides, axis=1)
+
+    def sort_own(which, carry):
+        span, value = sorted_part(core, which)
+        partial[span, :] = value
+        return carry
+
+    lax.fori_loop(0, strips, sort_own, 0, unroll=2)
     theirs = feats.at[1 - core]
     remote(theirs, theirs, s9.at[0], r9.at[0], sibling, h).wait_recv()
-    points = jnp.concatenate([feats[0], feats[1]], axis=1)
-    batch = 16
-    strip = batch * CAP
-    strips = chips // batch
-    own = chip // batch
-    spot = lax.broadcasted_iota(jnp.int32, (strip, 2 * rows), 0)
-    nt = (((1,), (1,)), ((), ()))
 
     def sort(i, carry):
         which = lax.rem(own + i, strips)
-        sides = []
-        for e in range(2):
-            onehot = (spot + which * strip == pick[e : e + 1, :]).astype(F32).astype(BF16)
-            sides.append(lax.dot_general(onehot, points, nt, preferred_element_type=F32))
-        both = jnp.concatenate(sides, axis=1).astype(BF16)
+        span, value = sorted_part(1 - core, which)
+        both = (partial[span, :] + value).astype(BF16)
         going[pl.ds(which * batch, batch)] = both.reshape(batch, CAP, 2 * width)
 
         def send(j, c):
@@ -444,10 +474,12 @@
         parts.append(two.T.astype(BF16))
     packed = jnp.concatenate(parts, axis=1)
     half = CAP * chips
-    total = jnp.dot(packed[:width], turned[:half, :], preferred_element_type=F32)
-    total += jnp.dot(packed[width:], turned[half:, :], preferred_element_type=F32)
-    moved[...] = total.astype(BF16)
-    gather_start(1, moved)
+    for j in order:
+        cols = slice(j * REACH, (j + 1) * REACH)
+        total = jnp.dot(packed[:width], turned[:half, cols], preferred_element_type=F32)
+        total += jnp.dot(packed[width:], turned[half:, cols], preferred_element_type=F32)
+        moved[:, cols] = total.astype(BF16)
+        gather_piece(1, moved, j)
     tables[1, mine, REACH : REACH + rows] = moved[...]
     run_block(1)
     out[...] = project(1)
@@ -481,8 +513,10 @@
             vmem((2, rows), jnp.int32),
             vmem((2, TAPS, width, channels), BF16),
             vmem((2, 3, width, channels), BF16),
-            vmem((2, channels, channels), BF16),
-            vmem((2, channels, channels), BF16),
+            vmem((2, width, channels), BF16),
+            vmem((channels, 2 * width), BF16),
+            vmem((groups, width, 2 * width), BF16),
+            vmem((2, width, channels), BF16),
             vmem((TAPS, blocks + 2, width, REACH), BF16),
             vmem((rows, 2 * width), BF16),
             vmem((heads, 2 * width, rows), BF16),
@@ -491,7 +525,8 @@
             vmem((lines, side, side, LANES), jnp.int32),
             vmem((2, width, rows), BF16),
             vmem((LANES, LANES), BF16),
-            vmem((2, 2 * rows), jnp.int32),
+            vmem((2, 2, chips * CAP, rows), BF16),
+            vmem((chips * CAP, 2 * width), F32),
             vmem((chips, CAP, 2 * width), BF16),
             vmem((chips, CAP, 2 * width), BF16),
             vmem((lines, chips, LANES), F32),

time: 93.5 us -> 93.2 us (level)
  no operation moved by 1% of the time
where the time goes in v5:
time: 93.2 us; the launch traced here: 93.1 us
  Pallas kernels  91.5 us (98%)
  local copies, waits for them, and re-layouts  1.57 us (2%)
    pallas_call x1, Pallas kernels, body(): pl.pallas_call(kernel, out_shape=jax.ShapeDtypeStruct((width, rows), BF16...  91.5 us

profile of v5, /device:TPU:1, one launch (start us, length us, event | category | flops | bytes accessed | tf_op | source)
XLA Modules:
  0.0 93.1 jit_solution(8518366608922095448)
XLA Ops:
  0.0 91.5 %blocks.1 = bf16[64,1024]{1,0:T(8,128)(2,1)} custom-call(bf16[64,1024]{1,0:T(8,128)(2,1)} %x.1, s32[27,2,1024]{2,1,0:T(2,128)} %bitcast.2, s32[2,1024]{1,0:T(2,128)} %valid.1, bf16[2,27,64,256]{3,2,1,0:T(8,128)(2,1)} %cw.1, bf16[2,3,64,256]{3,2,1,0:T(8,128)(2,1)} %aw.1, bf16[2,64,256]{2,1,0:T(8,128)(2,1)} %pw.1, s32[8,128]{1,0:T(8,128)} %bitcast.3), custom_call_target="tpu_custom_call" | custom-call | tf_op jit(solution)/shard_map/blocks/pallas_call | solution.py:503
  91.5 1.6 %copy.9 = bf16[64,1024]{1,0:T(8,128)(2,1)} copy(bf16[64,1024]{1,0:T(8,128)(2,1)} %blocks.1) | data formatting | bytes 262144

commit v6 on v5

--- a/solution.py
+++ b/solution.py
@@ -58,6 +58,8 @@
     feats,
     tri,
     onehot,
+    side_of,
+    turned_feats,
     partial,
     going,
     come,
@@ -142,19 +144,7 @@
     ]
     for load in loads:
         load.start()
-    low = lax.broadcasted_iota(jnp.int32, (LANES, LANES), 0)
-    high = lax.broadcasted_iota(jnp.int32, (LANES, LANES), 1)
-    tri[...] = jnp.where(low <= high, 1.0, 0.0).astype(BF16)
-    position = lax.broadcasted_iota(jnp.int32, (REACH, REACH), 0).astype(F32).astype(BF16)
-    one, zero = jnp.ones((), BF16), jnp.zeros((), BF16)
-    ones = jnp.where(lax.broadcasted_iota(jnp.int32, (HD, rows), 0) == 0, 1.0, 0.0).astype(BF16)
-    qm[...] = jnp.zeros(qm.shape, BF16)
-    for hd in range(heads):
-        qm[hd, width : width + HD, :] = ones
-        va[hd, HD:, :] = ones
     pl.semaphore_wait(barrier, chips - 1 + groups - 1 + 2)
-
-    order = (0, blocks - 1, *range(1, blocks - 1))
 
     def gather_piece(b, source, j):
         for d, other in enumerate(peers):
@@ -245,11 +235,10 @@
         for c in range(2):
             targets = jnp.concatenate([t for t, _ in slots[c * half : (c + 1) * half]], axis=1)
             halves = jnp.concatenate([e for _, e in slots[c * half : (c + 1) * half]], axis=1)
-            for e in range(2):
-                wanted = jnp.where(halves == e, targets, -1)
-                for i in range(strips):
-                    rows_of = slice(i * strip, (i + 1) * strip)
-                    onehot[e, c, rows_of, :] = (spot == wanted - i * strip).astype(F32).astype(BF16)
+            side_of[c : c + 1, :] = halves
+            for i in range(strips):
+                rows_of = slice(i * strip, (i + 1) * strip)
+                onehot[c, rows_of, :] = (spot == targets - i * strip).astype(F32).astype(BF16)
 
     def run_block(b):
         table = tables.at[b]
@@ -265,16 +254,6 @@
             h,
         )
         ship(first)
-        gather_wait(b, blocks - 1)
-        last = remote(
-            table.at[:, pl.ds(rows, REACH)],
-            table.at[:, pl.ds(0, REACH)],
-            s2.at[b, 1],
-            r2.at[b, 1],
-            after,
-            h,
-        )
-        ship(last)
         if b == 0:
             places_along_y()
             for load in loads[1:5]:
@@ -308,27 +287,38 @@
                 ship(remote(mix.at[mine, cols], mix.at[mine, cols], s3.at[b, blk, d], r3.at[b, blk, d], s, other))
 
         products(1)
-        products(blocks)
         for tile in range(2, blocks):
             gather_wait(b, tile - 1)
             products(tile)
-        for blk in range(1, blocks - 1):
+        conv(1)
+        gather_wait(b, blocks - 1)
+        last = remote(
+            table.at[:, pl.ds(rows, REACH)],
+            table.at[:, pl.ds(0, REACH)],
+            s2.at[b, 1],
+            r2.at[b, 1],
+            after,
+            h,
+        )
+        ship(last)
+        products(blocks)
+        for blk in range(2, blocks - 1):
             conv(blk)
         if b == 0:
             places_across()
+        first.wait_recv()
+        products(blocks + 1)
+        conv(blocks - 1)
         last.wait_recv()
         products(0)
         conv(0)
-        first.wait_recv()
-        products(blocks + 1)
-        conv(blocks - 1)
         if b == 0:
             prepare()
 
         scale = 1.0 / HD**0.5
         bias = jnp.where(vm[b : b + 1, :] > 0, 0.0, -1e30)
         weights = a[b].reshape(3 * width, -1)
-        for blk in (*range(1, blocks - 1), 0, blocks - 1):
+        for blk in (*range(1, blocks), 0):
             cols = slice(blk * REACH, (blk + 1) * REACH)
             for d, other in enumerate(froms):
                 theirs = mix.at[part(other), cols]
@@ -377,9 +367,19 @@
         update = jnp.dot(pt[b], ho[...], preferred_element_type=F32)
         return (mix[mine, :].astype(F32) + update).astype(BF16)
 
-    for j in order:
+    for j in range(blocks):
         gather_piece(0, x, j)
     places_along_z()
+    low = lax.broadcasted_iota(jnp.int32, (LANES, LANES), 0)
+    high = lax.broadcasted_iota(jnp.int32, (LANES, LANES), 1)
+    tri[...] = jnp.where(low <= high, 1.0, 0.0).astype(BF16)
+    position = lax.broadcasted_iota(jnp.int32, (REACH, REACH), 0).astype(F32).astype(BF16)
+    one, zero = jnp.ones((), BF16), jnp.zeros((), BF16)
+    ones = jnp.where(lax.broadcasted_iota(jnp.int32, (HD, rows), 0) == 0, 1.0, 0.0).astype(BF16)
+    qm[...] = jnp.zeros(qm.shape, BF16)
+    for hd in range(heads):
+        qm[hd, width : width + HD, :] = ones
+        va[hd, HD:, :] = ones
     weights_start()
     loads[0].wait()
     run_block(0)
@@ -388,24 +388,27 @@
     swap = remote(feats.at[core], feats.at[core], s9.at[0], r9.at[0], sibling, h)
     ship(swap)
     own = chip // batch
-    nt = (((1,), (1,)), ((), ()))
+
+    def turn_points(c):
+        points = feats[c].astype(F32)
+        half_of = side_of[pl.ds(c, 1), :]
+        both = jnp.concatenate([jnp.where(half_of == e, points, 0.0) for e in range(2)], axis=0)
+        turned_feats[c] = both.T.astype(BF16)
 
     def sorted_part(c, which):
         span = pl.ds(pl.multiple_of(which * strip, strip), strip)
-        points = feats[c]
-        sides = [
-            lax.dot_general(onehot[e, c, span, :], points, nt, preferred_element_type=F32) for e in range(2)
-        ]
-        return span, jnp.concatenate(sides, axis=1)
+        return span, jnp.dot(onehot[c, span, :], turned_feats[c], preferred_element_type=F32)
 
     def sort_own(which, carry):
         span, value = sorted_part(core, which)
         partial[span, :] = value
         return carry
 
+    turn_points(core)
     lax.fori_loop(0, strips, sort_own, 0, unroll=2)
     theirs = feats.at[1 - core]
     remote(theirs, theirs, s9.at[0], r9.at[0], sibling, h).wait_recv()
+    turn_points(1 - core)
 
     def sort(i, carry):
         which = lax.rem(own + i, strips)
@@ -474,7 +477,7 @@
         parts.append(two.T.astype(BF16))
     packed = jnp.concatenate(parts, axis=1)
     half = CAP * chips
-    for j in order:
+    for j in range(blocks):
         cols = slice(j * REACH, (j + 1) * REACH)
         total = jnp.dot(packed[:width], turned[:half, cols], preferred_element_type=F32)
         total += jnp.dot(packed[width:], turned[half:, cols], preferred_element_type=F32)
@@ -525,7 +528,9 @@
             vmem((lines, side, side, LANES), jnp.int32),
             vmem((2, width, rows), BF16),
             vmem((LANES, LANES), BF16),
-            vmem((2, 2, chips * CAP, rows), BF16),
+            vmem((2, chips * CAP, rows), BF16),
+            vmem((2, rows), jnp.int32),
+            vmem((2, rows, 2 * width), BF16),
             vmem((chips * CAP, 2 * width), F32),
             vmem((chips, CAP, 2 * width), BF16),
             vmem((chips, CAP, 2 * width), BF16),

time: 93.2 us -> 92 us (0.987)
  Pallas kernels: 91.5 us -> 90.2 us
    pallas_call x1, Pallas kernels: 91.5 us -> 90.2 us  [body(): pl.pallas_call(kernel, out_shape=jax.ShapeDtypeStruct((width, rows), BF16...]
where the time goes in v6:
time: 92 us; the launch traced here: 91.8 us
  Pallas kernels  90.2 us (98%)
  local copies, waits for them, and re-layouts  1.57 us (2%)
    pallas_call x1, Pallas kernels, body(): pl.pallas_call(kernel, out_shape=jax.ShapeDtypeStruct((width, rows), BF16...  90.2 us

profile of v6, /device:TPU:1, one launch (start us, length us, event | category | flops | bytes accessed | tf_op | source)
XLA Modules:
  0.0 91.8 jit_solution(8208732215714620365)
XLA Ops:
  0.0 90.2 %blocks.1 = bf16[64,1024]{1,0:T(8,128)(2,1)} custom-call(bf16[64,1024]{1,0:T(8,128)(2,1)} %x.1, s32[27,2,1024]{2,1,0:T(2,128)} %bitcast.2, s32[2,1024]{1,0:T(2,128)} %valid.1, bf16[2,27,64,256]{3,2,1,0:T(8,128)(2,1)} %cw.1, bf16[2,3,64,256]{3,2,1,0:T(8,128)(2,1)} %aw.1, bf16[2,64,256]{2,1,0:T(8,128)(2,1)} %pw.1, s32[8,128]{1,0:T(8,128)} %bitcast.3), custom_call_target="tpu_custom_call" | custom-call | tf_op jit(solution)/shard_map/blocks/pallas_call | solution.py:506
  90.3 1.6 %copy.9 = bf16[64,1024]{1,0:T(8,128)(2,1)} copy(bf16[64,1024]{1,0:T(8,128)(2,1)} %blocks.1) | data formatting | bytes 262144

commit v7 on v6

--- a/solution.py
+++ b/solution.py
@@ -37,10 +37,12 @@
     aw,
     pw,
     place,
-    out,
+    heads_last,
+    mix_out,
+    weight_out,
     tables,
     mixes,
-    heads_out,
+    heads_first,
     nb,
     vm,
     w,
@@ -90,8 +92,10 @@
     s10,
     r10,
 ):
-    width, rows = out.shape
+    width, rows = mix_out.shape
     heads = width // HD
+    heads_out = (heads_first, heads_last)
+    steps = [(0, 0, rows // 2), (0, rows // 2, rows // 2)] + [(hd, 0, rows) for hd in range(1, heads)]
     groups = lax.axis_size("head")
     shards = lax.axis_size("seq")
     side = places.shape[0]
@@ -243,7 +247,7 @@
     def run_block(b):
         table = tables.at[b]
         mix = mixes.at[b]
-        ho = heads_out.at[b]
+        ho = heads_out[b]
         gather_wait(b, 0)
         first = remote(
             table.at[:, pl.ds(REACH, REACH)],
@@ -312,8 +316,6 @@
         last.wait_recv()
         products(0)
         conv(0)
-        if b == 0:
-            prepare()
 
         scale = 1.0 / HD**0.5
         bias = jnp.where(vm[b : b + 1, :] > 0, 0.0, -1e30)
@@ -340,32 +342,30 @@
             keys = jnp.concatenate([qkv[width : 2 * width], tail], axis=0)
             kt[cols, :] = keys.T.astype(BF16)
 
-        def score(hd):
-            return jnp.dot(kt[...], qm[hd], preferred_element_type=F32)
+        def score(i):
+            hd, low, size = steps[i]
+            return jnp.dot(kt[...], qm[hd, :, low : low + size], preferred_element_type=F32)
 
         upcoming = score(0)
-        for hd in range(heads):
+        for i, (hd, low, size) in enumerate(steps):
             scores = upcoming
-            if hd + 1 < heads:
-                upcoming = score(hd + 1)
+            if i + 1 < len(steps):
+                upcoming = score(i + 1)
             top = jnp.max(scores, axis=0, keepdims=True)
             probs = jnp.exp(scores - top).astype(BF16)
             summed = jnp.dot(va[hd], probs, preferred_element_type=F32)
             result = summed[:HD] / summed[HD : HD + 1]
             span = part(h, HD, hd * HD)
-            ho[span, :] = result.astype(BF16)
+            ho[span, low : low + size] = result.astype(BF16)
             for d, other in enumerate(peers):
-                ship(remote(ho.at[span, :], ho.at[span, :], s4.at[b, hd, d], r4.at[b, hd, d], s, other))
-
-    def project(b):
-        mix = mixes.at[b]
-        ho = heads_out.at[b]
-        for hd in range(heads):
+                piece = ho.at[span, pl.ds(low, size)]
+                ship(remote(piece, piece, s4.at[b, i, d], r4.at[b, i, d], s, other))
+
+    def heads_wait(b):
+        for i, (hd, low, size) in enumerate(steps):
             for d, other in enumerate(froms):
-                theirs = ho.at[part(other, HD, hd * HD), :]
-                remote(theirs, theirs, s4.at[b, hd, d], r4.at[b, hd, d], s, other).wait_recv()
-        update = jnp.dot(pt[b], ho[...], preferred_element_type=F32)
-        return (mix[mine, :].astype(F32) + update).astype(BF16)
+                theirs = heads_out[b].at[part(other, HD, hd * HD), pl.ds(low, size)]
+                remote(theirs, theirs, s4.at[b, i, d], r4.at[b, i, d], s, other).wait_recv()
 
     for j in range(blocks):
         gather_piece(0, x, j)
@@ -383,8 +383,11 @@
     weights_start()
     loads[0].wait()
     run_block(0)
-
-    feats[core] = project(0)
+    prepare()
+
+    heads_wait(0)
+    update = jnp.dot(pt[0], heads_out[0][...], preferred_element_type=F32)
+    feats[core] = (mixes[0, mine, :].astype(F32) + update).astype(BF16)
     swap = remote(feats.at[core], feats.at[core], s9.at[0], r9.at[0], sibling, h)
     ship(swap)
     own = chip // batch
@@ -485,7 +488,9 @@
         gather_piece(1, moved, j)
     tables[1, mine, REACH : REACH + rows] = moved[...]
     run_block(1)
-    out[...] = project(1)
+    mix_out[...] = mixes[1, mine, :]
+    weight_out[...] = pt[1]
+    heads_wait(1)
     for copy in sends:
         copy.wait_send()
     every.wait_send()
@@ -501,17 +506,21 @@
     others = groups - 1
     dma = pltpu.SemaphoreType.DMA
     vmem = pltpu.VMEM
-    pairs = [(2, blocks, others), (2, 2), (2, blocks, others), (2, heads, others), (others,)]
+    pairs = [(2, blocks, others), (2, 2), (2, blocks, others), (2, heads + 1, others), (others,)]
     pairs += [(side - 1,), (side - 1,), (1,), (1,), (1,)]
-    return pl.pallas_call(
+    heads_all, mixed, weight = pl.pallas_call(
         kernel,
-        out_shape=jax.ShapeDtypeStruct((width, rows), BF16),
+        out_shape=[
+            jax.ShapeDtypeStruct((channels, rows), BF16),
+            jax.ShapeDtypeStruct((width, rows), BF16),
+            jax.ShapeDtypeStruct((width, channels), BF16),
+        ],
         in_specs=[pl.BlockSpec(memory_space=pl.ANY)] * 7,
-        out_specs=pl.BlockSpec(memory_space=pltpu.VMEM),
+        out_specs=[pl.BlockSpec(memory_space=pltpu.VMEM)] * 3,
         scratch_shapes=[
             vmem((2, channels, rows + 2 * REACH), BF16),
             vmem((2, channels, rows), BF16),
-            vmem((2, channels, rows), BF16),
+            vmem((channels, rows), BF16),
             vmem((TAPS, 2, rows), jnp.int32),
             vmem((2, rows), jnp.int32),
             vmem((2, TAPS, width, channels), BF16),
@@ -555,6 +564,8 @@
         proj_weight,
         hilbert_place.reshape(rows // LANES, LANES),
     )
+    update = jnp.dot(weight, heads_all, preferred_element_type=F32)
+    return (mixed.astype(F32) + update).astype(BF16)
 
 
 def solution(mesh):

time: 92 us -> 92.7 us (level)
  matrix products: 0 us -> 1.95 us
  local copies, waits for them, and re-layouts: 1.57 us -> 0 us
    dot_general x0 -> x1, matrix products: none -> 1.95 us  [body(): update = jnp.dot(weight, heads_all, preferred_element_type=F32)]
    unnamed x1 -> x0, local copies, waits for them, and re-layouts: 1.57 us -> none
where the time goes in v7:
time: 92.7 us; the launch traced here: 92.5 us
  Pallas kernels  90.6 us (98%)
  matrix products  1.95 us (2%)
    pallas_call x1, Pallas kernels, body(): pl.pallas_call(kernel, out_shape=[jax.ShapeDtypeStruct((channels, rows),...  90.6 us
    dot_general x1, matrix products, body(): update = jnp.dot(weight, heads_all, preferred_element_type=F32)  1.95 us

profile of v7, /device:TPU:1, one launch (start us, length us, event | category | flops | bytes accessed | tf_op | source)
XLA Modules:
  0.0 92.5 jit_solution(5643379324731110816)
XLA Ops:
  0.0 90.6 %blocks.1 = (bf16[256,1024]{1,0:T(8,128)(2,1)}, bf16[64,1024]{1,0:T(8,128)(2,1)}, bf16[64,256]{1,0:T(8,128)(2,1)}) custom-call(bf16[64,1024]{1,0:T(8,128)(2,1)} %x.1, s32[27,2,1024]{2,1,0:T(2,128)} %bitcast.4, s32[2,1024]{1,0:T(2,128)} %valid.1, bf16[2,27,64,256]{3,2,1,0:T(8,128)(2,1)} %cw.1, bf16[2,3,64,256]{3,2,1,0:T(8,128)(2,1)} %aw.1, ...), custom_call_target="tpu_custom_call" | custom-call | tf_op jit(solution)/shard_map/blocks/pallas_call | solution.py:511
  90.6 1.9 %fusion = bf16[64,1024]{1,0:T(8,128)(2,1)} fusion(bf16[64,256]{1,0:T(8,128)(2,1)} %get-tuple-element.9, bf16[256,1024]{1,0:T(8,128)(2,1)} %get-tuple-element.10, bf16[64,1024]{1,0:T(8,128)(2,1)} %get-tuple-element.8), kind=kOutput, calls=%fused_computation.1 | convolution fusion | flops 33751040 | bytes 819200 | tf_op jit(solution)/shard_map/dot_general | solution.py:567

commit v8 on v6

--- a/solution.py
+++ b/solution.py
@@ -132,7 +132,6 @@
         pl.semaphore_signal(barrier, inc=1, device_id=(s, other), device_id_type=MESH)
     for other in (before, after):
         pl.semaphore_signal(barrier, inc=1, device_id=(other, h), device_id_type=MESH)
-    lax.fori_loop(1, chips, greet, 0)
     loads = [
         pltpu.make_async_copy(x, tables.at[0, mine, pl.ds(REACH, rows)], local.at[0]),
         pltpu.make_async_copy(cw, w, local.at[1]),
@@ -144,6 +143,7 @@
     ]
     for load in loads:
         load.start()
+    lax.fori_loop(1, chips, greet, 0, unroll=7)
     pl.semaphore_wait(barrier, chips - 1 + groups - 1 + 2)
 
     def gather_piece(b, source, j):
@@ -312,8 +312,6 @@
         last.wait_recv()
         products(0)
         conv(0)
-        if b == 0:
-            prepare()
 
         scale = 1.0 / HD**0.5
         bias = jnp.where(vm[b : b + 1, :] > 0, 0.0, -1e30)
@@ -383,6 +381,7 @@
     weights_start()
     loads[0].wait()
     run_block(0)
+    prepare()
 
     feats[core] = project(0)
     swap = remote(feats.at[core], feats.at[core], s9.at[0], r9.at[0], sibling, h)

time: 92 us -> 91.3 us (level)
  no operation moved by 1% of the time
where the time goes in v8:
time: 91.3 us; the launch traced here: 91.1 us
  Pallas kernels  89.5 us (98%)
  local copies, waits for them, and re-layouts  1.57 us (2%)
    pallas_call x1, Pallas kernels, body(): pl.pallas_call(kernel, out_shape=jax.ShapeDtypeStruct((width, rows), BF16...  89.5 us

profile of v8, /device:TPU:1, one launch (start us, length us, event | category | flops | bytes accessed | tf_op | source)
XLA Modules:
  0.0 91.1 jit_solution(12368287175145886508)
XLA Ops:
  0.0 89.5 %blocks.1 = bf16[64,1024]{1,0:T(8,128)(2,1)} custom-call(bf16[64,1024]{1,0:T(8,128)(2,1)} %x.1, s32[27,2,1024]{2,1,0:T(2,128)} %bitcast.2, s32[2,1024]{1,0:T(2,128)} %valid.1, bf16[2,27,64,256]{3,2,1,0:T(8,128)(2,1)} %cw.1, bf16[2,3,64,256]{3,2,1,0:T(8,128)(2,1)} %aw.1, bf16[2,64,256]{2,1,0:T(8,128)(2,1)} %pw.1, s32[8,128]{1,0:T(8,128)} %bitcast.3), custom_call_target="tpu_custom_call" | custom-call | tf_op jit(solution)/shard_map/blocks/pallas_call | solution.py:505
  89.5 1.6 %copy.9 = bf16[64,1024]{1,0:T(8,128)(2,1)} copy(bf16[64,1024]{1,0:T(8,128)(2,1)} %blocks.1) | data formatting | bytes 262144
